TPU v7x, 128 devices: a whole 4x4x4 slice. The times are simulated.
128 devices in a mesh: dp: 32 (over x, z, core), col: 4 (over y).
Axes of the slice: x: 4, y: 4, z: 4, core: 2. Of those that a mesh axis runs over, the one named last changes fastest.
Arguments:
- act: bfloat16 [8192, 4096], P('dp'), may hold values from -6 to 6
- grad: bfloat16 [8192, 4096], P('dp'), may hold values from -6 to 6
- lengths: int32 [64], P('dp'), may hold values from 1 to 128, 6144 in all
- basis_in: bfloat16 [4096, 4096], P(None, 'col')
- basis_out: bfloat16 [4096, 4096], P(None, 'col')
- query_act: bfloat16 [1024, 4096], P('dp'), may hold values from -6 to 6
- query_grad: bfloat16 [1024, 4096], P('dp'), may hold values from -6 to 6
Outputs:
- scores: float32 [64, 32], P('dp')
All inputs are finite; a program needn't handle non-finite values. No bound on the sum of `lengths` on one device may be relied on, other than what follows from the above.
Results may differ from a plain program's by a relative error of at most 0.0015.
The roundings to bfloat16 on the way count: a program that leaves them out, or rounds other values in their place, can miss the bound.
Values may be sent and summed in bfloat16 or wider, within the bound.
A program may use at most 192 MiB of HBM per device.

v0:
```python
import jax
import jax.numpy as jnp
from jax import lax
from jax.sharding import PartitionSpec as P

DI = 4096
DO = 4096
RANK = 32
RLEN = 128


damping_share = 0.1
ridge_share = 0.05
epsilon_add = 1e-06


def solve_rank(left_rows, projected, ridge_eye):
    gram = (
        jnp.einsum("qrg,qsg->qrs", left_rows, left_rows, preferred_element_type=jnp.float32)
        + ridge_eye
    )
    factor = jnp.linalg.cholesky(gram)
    middle = lax.linalg.triangular_solve(factor, projected, left_side=True, lower=True)
    return lax.linalg.triangular_solve(factor, middle, left_side=True, lower=True, transpose_a=True)


def shards(act, grad, lengths, basis_in, basis_out, query_act, query_grad):
    resp_dev = lengths.shape[0]
    tok_dev = act.shape[0]
    inner_width = basis_in.shape[1]
    col_count = lax.axis_size("col")
    dp_count = lax.axis_size("dp")
    live_mask = (
        (jnp.arange(RLEN, dtype=jnp.int32)[None, :] < lengths[:, None])
        .reshape(tok_dev, 1)
        .astype(jnp.bfloat16)
    )
    masked = grad * live_mask
    rot_in = jnp.dot(act, basis_in, preferred_element_type=jnp.float32).astype(jnp.bfloat16)
    out_part = jnp.dot(masked, basis_out, preferred_element_type=jnp.float32).astype(jnp.bfloat16)
    query_in = jnp.dot(query_act, basis_in, preferred_element_type=jnp.float32).astype(jnp.bfloat16)
    query_part = jnp.dot(query_grad, basis_out, preferred_element_type=jnp.float32).astype(
        jnp.bfloat16
    )
    rot_out, in_full, query_out = (
        lax.all_gather(out_part, "col", axis=1, tiled=True),
        lax.all_gather(rot_in, "col", axis=1, tiled=True),
        lax.all_gather(query_part, "col", axis=1, tiled=True),
    )
    query_all = lax.all_gather(query_out, "dp", axis=0, tiled=True)
    squares = jnp.zeros((DO, inner_width), jnp.float32)
    for member in range(resp_dev):
        grad_rows = rot_out[member * RLEN : (member + 1) * RLEN]
        act_rows = rot_in[member * RLEN : (member + 1) * RLEN]
        product = lax.dot_general(
            grad_rows, act_rows, (((0,), (0,)), ((), ())), preferred_element_type=jnp.float32
        )
        squares = squares + product * product
    partial_value = squares / (resp_dev * dp_count)
    ridge_eye = ridge_share * DO * jnp.eye(RANK, dtype=jnp.float32)
    in_split = in_full.reshape(tok_dev, col_count, inner_width)
    corr = lax.psum(partial_value, "dp")
    grand_sum = lax.psum(jnp.sum(corr), "col")
    damping_add = damping_share * grand_sum / (DO * DI) + epsilon_add
    query_count = query_out.shape[0] // RANK
    query_left = query_out.reshape(query_count, RANK, DO)
    query_right = query_in.reshape(query_count, RANK, inner_width)
    rotated = jnp.einsum(
        "qrg,qra->qga", query_left, query_right, preferred_element_type=jnp.float32
    )
    scaled = (rotated / (corr + damping_add)).astype(jnp.bfloat16)
    projected = jnp.einsum("qrg,qga->qra", query_left, scaled, preferred_element_type=jnp.float32)
    solved = solve_rank(query_left, projected, ridge_eye).astype(jnp.bfloat16)
    pieces = lax.all_gather(solved, ("dp", "col"), axis=0, tiled=True)
    pieces = pieces.reshape(dp_count, col_count, query_count * RANK, inner_width)
    right_side = jnp.einsum(
        "tca,dcma->tdm", in_split, pieces, preferred_element_type=jnp.float32
    ).reshape(tok_dev, -1)
    left_side = lax.dot_general(
        rot_out, query_all, (((1,), (1,)), ((), ())), preferred_element_type=jnp.float32
    )
    joined = (left_side * right_side).reshape(tok_dev, -1, RANK).sum(axis=2)
    return joined.reshape(resp_dev, RLEN, -1).sum(axis=1) / RLEN


def solution(mesh):
    return jax.shard_map(
        shards,
        mesh=mesh,
        in_specs=(
            P("dp", None),
            P("dp", None),
            P("dp"),
            P(None, "col"),
            P(None, "col"),
            P("dp", None),
            P("dp", None),
        ),
        out_specs=P("dp", None),
        check_vma=False,
    )
```

profile of v0, /device:TPU:1, one launch (start us, length us, event | category | flops | bytes accessed | tf_op | source)
XLA Modules:
  0.0 415.3 jit_solution(15832137899388951141)
XLA Ops:
  6.5 0.9 fusion.28
  7.4 7.2 %fusion.14 = bf16[256,1024]{1,0:T(8,128)(2,1)} fusion(bf16[4096,1024]{1,0:T(8,128)(2,1)} %param.11, bf16[256,4096]{1,0:T(8,128)(2,1)} %param.8, bf16[256]{0:T(256)(128)(2,1)S(1)} %fusion.28), kind=kOutput, calls=%fused_computation.11 | convolution fusion | flops 2148794368 | bytes 11010560 | tf_op jit(solution)/shard_map/dot_general | solution.py:40
  14.7 5.7 %convolution_convert_fusion = bf16[256,1024]{1,0:T(8,128)(2,1)S(1)} fusion(bf16[256,4096]{1,0:T(8,128)(2,1)S(1)} %copy-done, bf16[4096,1024]{1,0:T(8,128)(2,1)} %param.10), kind=kOutput, calls=%fused_computation.12 | convolution fusion | flops 2147745792 | bytes 11010048 | tf_op jit(solution)/shard_map/dot_general | solution.py:39
  20.4 28.4 %all-gather.6.cloned.1.call-done = bf16[256,4096]{1,0:T(8,128)(2,1)} async-done(((bf16[256,1024]{1,0:T(8,128)(2,1)}), bf16[256,4096]{1,0:T(8,128)(2,1)}) %all-gather.6.cloned.1.call-update) | async-done | bytes 2097168 | tf_op jit(solution)/shard_map/all_gather | solution.py:46
  48.8 3.7 fusion.18
  52.6 7.1 %add_multiply_fusion = f32[4096,1024]{1,0:T(8,128)} fusion(f32[4096,1024]{1,0:T(8,128)S(1)} %fusion.18, bf16[256,4096]{1,0:T(8,128)(2,1)S(1)} %copy-done.2, bf16[256,1024]{1,0:T(8,128)(2,1)S(1)} %convolution_convert_fusion), kind=kOutput, calls=%fused_computation.1 | convolution fusion | flops 1090519040 | bytes 34865152 | tf_op jit(solution)/shard_map/dot_general | solution.py:55
  59.8 0.9 copy-done.5
  60.7 4.9 %convolution_convert_fusion.2 = bf16[32,1024]{1,0:T(8,128)(2,1)S(1)} fusion(bf16[32,4096]{1,0:T(8,128)(2,1)S(1)} %copy-done.5, bf16[4096,1024]{1,0:T(8,128)(2,1)} %param.11), kind=kOutput, calls=%fused_computation.14 | convolution fusion | flops 268468224 | bytes 8716288 | tf_op jit(solution)/shard_map/dot_general | solution.py:42
  65.6 10.7 %all_gather.16 = bf16[32,4096]{1,0:T(8,128)(2,1)} all-gather(bf16[32,1024]{1,0:T(8,128)(2,1)S(1)} %convolution_convert_fusion.2), channel_id=1, replica_groups=mesh['dp'=32,'col'=4] {'col'}, dimensions={1}, use_global_device_ids=true | all-gather | bytes 327680 | tf_op jit(solution)/shard_map/all_gather | solution.py:48
  76.3 0.2 all-gather.12.cloned.1.call-start
  76.5 1.2 convolution_add_fusion
  77.9 2.9 custom-call.9
  80.8 0.6 compare_reduce_fusion
  81.5 0.7 fusion.23
  82.1 5.2 %convolution_convert_fusion.1 = bf16[32,1024]{1,0:T(8,128)(2,1)S(1)} fusion(bf16[32,4096]{1,0:T(8,128)(2,1)S(1)} %copy-done.6, bf16[4096,1024]{1,0:T(8,128)(2,1)} %param.10), kind=kOutput, calls=%fused_computation.13 | convolution fusion | flops 268468224 | bytes 8716288 | tf_op jit(solution)/shard_map/dot_general | solution.py:41
  87.3 151.8 %all-reduce.2.cloned.1.call-done = f32[4096,1024]{1,0:T(8,128)} async-done(((f32[4096,1024]{1,0:T(8,128)}), f32[4096,1024]{1,0:T(8,128)}) %all-reduce.2.cloned.1.call-update) | async-done | bytes 16777232 | tf_op jit(solution)/shard_map/psum | solution.py:62
  239.1 10.7 %reduce_sum.27 = f32[]{:T(128)} reduce(f32[4096,1024]{1,0:T(8,128)} %all-reduce.2.cloned.1.call-done, f32[]{:T(128)} %constant.57.clone.1), dimensions={0,1}, to_apply=%region_3.4 | reduce | flops 4194303 | bytes 16777224 | tf_op jit(solution)/shard_map/reduce_sum | solution.py:63
  249.8 2.5 custom-call.10
  252.2 9.5 %psum.15 = f32[]{:T(128)} all-reduce(f32[]{:T(128)} %reduce_sum.27), channel_id=1, replica_groups=mesh['dp'=32,'col'=4] {'col'}, use_global_device_ids=true, to_apply=%region_4.5 | all-reduce | flops 1 | bytes 8 | tf_op jit(solution)/shard_map/psum | solution.py:63
  262.4 9.7 %fusion = f32[32,1024]{1,0:T(8,128)S(1)} fusion(bf16[32,4096]{1,0:T(8,128)(2,1)S(1)} %copy-done.3, f32[4096,1024]{1,0:T(8,128)} %all-reduce.2.cloned.1.call-done, f32[]{:T(128)S(6)} %add.39, bf16[32,1024]{1,0:T(8,128)(2,1)S(1)} %convolution_convert_fusion.1), kind=kOutput, calls=%fused_computation.2 | convolution fusion | flops 549453824 | bytes 17235972 | tf_op jit(solution)/shard_map/qrg,qga->qra/dot_general | solution.py:72
  272.0 0.3 fusion.26
  272.4 0.9 convolution_convert_fusion.3
  273.3 0.3 all-gather.10.cloned.1.call-start
  273.6 0.3 all-gather.10.cloned.1.call-update
  273.9 22.1 %all-gather.8.cloned.1.call-done = bf16[1024,4096]{1,0:T(8,128)(2,1)} async-done(((bf16[32,4096]{1,0:T(8,128)(2,1)}), bf16[1024,4096]{1,0:T(8,128)(2,1)}) %all-gather.8.cloned.1.call-update) | async-done | bytes 8388624 | tf_op jit(solution)/shard_map/all_gather | solution.py:50
  296.0 5.7 %fusion.29 = f32[256,1024]{1,0:T(8,128)S(1)} fusion(bf16[256,4096]{1,0:T(8,128)(2,1)S(1)} %copy-done.2, bf16[1024,4096]{1,0:T(8,128)(2,1)} %all-gather.8.cloned.1.call-done), kind=kOutput, calls=%fused_computation.39 | convolution fusion | flops 2147483648 | bytes 11534336 | tf_op jit(solution)/shard_map/dot_general | solution.py:79
  301.7 67.4 %all-gather.12.cloned.1.call-done = bf16[4096,1024]{1,0:T(8,128)(2,1)} async-done(((bf16[32,1024]{1,0:T(8,128)(2,1)}), bf16[4096,1024]{1,0:T(8,128)(2,1)}) %all-gather.12.cloned.1.call-update) | async-done | bytes 8388624 | tf_op jit(solution)/shard_map/all_gather | solution.py:74
  369.2 8.5 %copy.30 = bf16[32,32,1024,4]{2,1,0,3:T(8,128)(2,1)} copy(bf16[32,32,1024,4]{2,1,3,0:T(8,128)(2,1)} %bitcast.52) | data formatting | bytes 16777216 | tf_op jit(solution)/shard_map/tca,dcma->tdm/dot_general | solution.py:76
  377.6 21.1 %all-gather.10.cloned.1.call-done = bf16[256,4096]{1,0:T(8,128)(2,1)} async-done(((bf16[256,1024]{1,0:T(8,128)(2,1)}), bf16[256,4096]{1,0:T(8,128)(2,1)}) %all-gather.10.cloned.1.call-update) | async-done | bytes 2097168 | tf_op jit(solution)/shard_map/all_gather | solution.py:47
  398.7 7.5 %fusion.11 = f32[256,1024]{1,0:T(8,128)} fusion(f32[256,1024]{1,0:T(8,128)S(1)} %fusion.29, bf16[1024,1024,4]{1,0,2:T(8,128)(2,1)} %bitcast.53, bf16[32,4,8,1024]{3,2,1,0:T(8,128)(2,1)} %bitcast.55), kind=kOutput, calls=%fused_computation.10 | convolution fusion | flops 2147745792 | bytes 12582912 | tf_op jit(solution)/shard_map/tca,dcma->tdm/dot_general | solution.py:76
  406.2 1.6 copy.32
  408.1 0.6 broadcast_multiply_fusion
  (27 shorter events, 0.6 us)
Async XLA Ops:
  6.5 8.1 %copy-start = (bf16[256,4096]{1,0:T(8,128)(2,1)S(1)}, bf16[256,4096]{1,0:T(8,128)(2,1)}, u32[]{:S(2)}) copy-start(bf16[256,4096]{1,0:T(8,128)(2,1)} %param.7) | copy-start | bytes 6291460
  6.5 42.3 %all-gather.6.cloned.1.call-start = ((), (), s32[]{:S(2)}) async-start(), calls=%async_computation | async-start | bytes 2621440 | tf_op jit(solution)/shard_map/all_gather | solution.py:46
  14.6 224.5 %all-reduce.2.cloned.1.call-start = ((), (), s32[]{:S(2)}) async-start(), calls=%async_computation.3 | async-start | bytes 33554432 | tf_op jit(solution)/shard_map/psum | solution.py:62
  20.4 32.2 %copy-start.4 = (bf16[256,1024]{1,0:T(8,128)(2,1)}, bf16[256,1024]{1,0:T(8,128)(2,1)S(1)}, u32[]{:S(2)}) copy-start(bf16[256,1024]{1,0:T(8,128)(2,1)S(1)} %convolution_convert_fusion) | copy-start | bytes 1572868
  48.8 3.8 copy-start.2
  59.7 0.9 copy-start.5
  59.7 22.4 %copy-start.6 = (bf16[32,4096]{1,0:T(8,128)(2,1)S(1)}, bf16[32,4096]{1,0:T(8,128)(2,1)}, u32[]{:S(2)}) copy-start(bf16[32,4096]{1,0:T(8,128)(2,1)} %param.12) | copy-start | bytes 786436
  59.8 236.2 %all-gather.8.cloned.1.call-start = ((), (), s32[]{:S(2)}) async-start(), calls=%async_computation.1 | async-start | bytes 8650752 | tf_op jit(solution)/shard_map/all_gather | solution.py:50
  76.3 292.8 %all-gather.12.cloned.1.call-start = ((), (), s32[]{:S(2)}) async-start(), calls=%async_computation.4 | async-start | bytes 8454144 | tf_op jit(solution)/shard_map/all_gather | solution.py:74
  87.3 175.1 %copy-start.3 = (bf16[32,4096]{1,0:T(8,128)(2,1)S(1)}, bf16[32,4096]{1,0:T(8,128)(2,1)}, u32[]{:S(2)}) copy-start(bf16[32,4096]{1,0:T(8,128)(2,1)} %all_gather.16) | copy-start | bytes 786436
  273.3 125.4 %all-gather.10.cloned.1.call-start = ((), (), s32[]{:S(2)}) async-start(), calls=%async_computation.2 | async-start | bytes 2621440 | tf_op jit(solution)/shard_map/all_gather | solution.py:47
  398.7 10.0 %copy-start.1 = (bf16[256,4096]{1,0:T(8,128)(2,1)S(1)}, bf16[256,4096]{1,0:T(8,128)(2,1)}, u32[]{:S(2)}) copy-start(bf16[256,4096]{1,0:T(8,128)(2,1)} %param.7) | copy-start | bytes 6291460
Sparse Core Ops, SparseCore 0:
  14.7 34.0 all-gather.5
  59.9 179.1 all-reduce.1
  241.6 54.3 all-gather.7
  299.4 69.6 all-gather.11
  370.8 27.9 all-gather.9
where the time goes:
time: 416 us; the launch traced here: 415 us
  waiting for transfers between devices  291 us (70%)
  matrix products  59.2 us (14%)
  blocking collectives  20.2 us (5%)
  other arithmetic  19.1 us (5%)
  between operations  13.9 us (3%)
  local copies, waits for them, and re-layouts  11.1 us (3%)
    psum x1, waiting for transfers between devices, shards(): corr = lax.psum(partial_value, 'dp')  152 us
    all_gather x1, waiting for transfers between devices, shards(): pieces = lax.all_gather(solved, ('dp', 'col'), axis=0, tiled=True)  67.4 us
    all_gather x1, waiting for transfers between devices, shards(): lax.all_gather(out_part, 'col', axis=1, tiled=True)  28.4 us
    all_gather x1, waiting for transfers between devices, shards(): query_all = lax.all_gather(query_out, 'dp', axis=0, tiled=True)  22.1 us
    all_gather x1, waiting for transfers between devices, shards(): lax.all_gather(rot_in, 'col', axis=1, tiled=True)  21.1 us
    dot_general x2, matrix products, shards(): lax.dot_general(grad_rows, act_rows, (((0,), (0,)), ((), ())), preferred_...  10.8 us
    all_gather x1, blocking collectives, shards(): lax.all_gather(query_part, 'col', axis=1, tiled=True)  10.7 us
    reduce_sum x1, other arithmetic, shards(): grand_sum = lax.psum(jnp.sum(corr), 'col')  10.7 us
  transfers between devices with their start and end apart: 5, of which 5 were waited for; matrix products, arithmetic and copies ran while one was open for 14% of the time, Pallas kernels for 0%

commit v1 on v0

v1 whole, which is shorter than its diff:
```python
import functools

import jax
import jax.numpy as jnp
from jax import lax
from jax.experimental import pallas as pl
from jax.experimental.pallas import tpu as pltpu
from jax.sharding import PartitionSpec as P


RLEN = 128
RANK = 32
DIM = 4096
WIDTH = 1024
TOK = 256
PARTS = 8
damping_share = 0.1
ridge_share = 0.05
epsilon_add = 1e-06
BF = jnp.bfloat16
F32 = jnp.float32
MESH = pl.DeviceIdType.MESH
HIGH = lax.Precision.HIGHEST


def dot(a, b, dims, precision=None):
    return lax.dot_general(a, b, (dims, ((), ())), preferred_element_type=F32, precision=precision)


NN = ((1,), (0,))
TN = ((0,), (0,))
NT = ((1,), (1,))


class Slots:
    def __init__(self):
        self.count = 0

    def take(self, n):
        first = self.count
        self.count += n
        return first


SL = Slots()
S_SWAP_I = SL.take(2)
S_SWAP_A = SL.take(1)
S_SWAP_G = SL.take(4)
S_Y_I = SL.take(6)
S_L1 = SL.take(3)
S_L2 = SL.take(3)
S_LS = SL.take(1)
S_A = SL.take(15)
S_AY = SL.take(3)
S_FAR = SL.take(2 * PARTS)
S_NEAR = SL.take(2 * PARTS)
S_FAR2 = SL.take(2 * PARTS)
S_NEAR2 = SL.take(2 * PARTS)
S_GRAM = SL.take(3)
S_LEFT = SL.take(3)
S_LEFTS = SL.take(1)
S_D1 = SL.take(7)
S_D2 = SL.take(15)
S_PROJ = SL.take(3)
S_S1 = SL.take(3)
S_S2 = SL.take(3)
S_FIN = SL.take(7)
N_SEM = SL.count


def kernel(
    act, grad, lens, b_in, b_out, q_act, q_grad,
    out,
    xin, xout, bin_, bout, send_i, ibuf, gbuf, lb, at_send, a_own, a_recv, a4,
    acc, snd, far, near, snd2, far2, near2, corr,
    gram_s, gram_r, left_s, left_r, left_f, damp_1, damp_2, inv_bd, proj_s, proj_r, sb, fin,
    load_sem, ss, rs,
):
    dp = lax.axis_index("dp")
    y = lax.axis_index("col")
    x, z, h = dp // 8, (dp // 2) % 4, dp % 2
    u = x * (1 - h) + z * h
    v = z * (1 - h) + x * h
    me = u * 4 + v

    def dev_xz(xx, zz, hh, yy):
        return ((xx % 4) * 8 + (zz % 4) * 2 + hh, yy % 4)

    def dev(du, dv):
        uu, vv = u + du, v + dv
        return dev_xz(uu * (1 - h) + vv * h, vv * (1 - h) + uu * h, h, y)

    def dev_y(dy, dh=0):
        return dev_xz(x, z, (h + dh) % 2, y + dy)

    sibling = dev_y(0, 1)
    pending = []

    def copy(src, dst, idx, to):
        return pltpu.make_async_remote_copy(
            src_ref=src, dst_ref=dst, send_sem=ss.at[idx], recv_sem=rs.at[idx], device_id=to, device_id_type=MESH
        )

    def send(src, dst, idx, to):
        c = copy(src, dst, idx, to)
        c.start()
        pending.append(c)

    def tile_in(k):
        half = (1 - h) * (1 - k // 2) + h * (k // 2)
        return half * 2 + k % 2

    def load_in(k):
        cols = pl.ds(pl.multiple_of(tile_in(k) * 256, 256), 256)
        return pltpu.make_async_copy(b_in.at[:, cols], bin_.at[k], load_sem.at[4 + k])

    def load_out(k):
        cols = pl.ds(pl.multiple_of(k * 256, 256), 256)
        return pltpu.make_async_copy(b_out.at[:, cols], bout.at[k], load_sem.at[8 + k])

    rows_of = [
        pltpu.make_async_copy(act, xin.at[pl.ds(0, TOK)], load_sem.at[0]),
        pltpu.make_async_copy(q_act, xin.at[pl.ds(TOK, RANK)], load_sem.at[1]),
        pltpu.make_async_copy(grad, xout.at[pl.ds(0, TOK)], load_sem.at[2]),
        pltpu.make_async_copy(q_grad, xout.at[pl.ds(TOK, RANK)], load_sem.at[3]),
    ]
    rows_of[0].start()
    rows_of[1].start()
    for k in range(4):
        load_in(k).start()
    rows_of[2].start()
    rows_of[3].start()
    for k in range(4):
        load_out(k).start()

    barrier = pltpu.get_barrier_semaphore()
    peers = [dev(du, dv) for du in range(4) for dv in range(4) if du or dv]
    peers += [dev_y(dy, dh) for dy in range(4) for dh in range(2) if dy or dh]
    for to in peers:
        pl.semaphore_signal(barrier, inc=1, device_id=to, device_id_type=MESH)
    pl.semaphore_wait(barrier, len(peers))

    lane = lax.broadcasted_iota(jnp.int32, (RANK, 128), 1)
    spread = (lane == lax.broadcasted_iota(jnp.int32, (RANK, 128), 0) + RANK * u).astype(BF)

    rows_of[0].wait()
    rows_of[1].wait()
    own_rows = pl.ds(pl.multiple_of(h * TOK, TOK), TOK)

    def swap_i(k):
        return copy(send_i.at[k], ibuf.at[k, own_rows], S_SWAP_I + k, sibling)

    def step_in(k, carry):
        load_in(k).wait()
        r = dot(xin[...], bin_[k], NN).astype(BF)
        at = dot(r[TOK:], spread, TN).astype(BF).reshape(16, 16, 128)

        @pl.when(k < 2)
        def _():
            send_i[k] = r[:TOK]
            at_send[k] = at
            swap_i(k).start()

        @pl.when(k >= 2)
        def _():
            ibuf[k - 2, own_rows] = r[:TOK]
            a_own[h, k - 2] = at

        return carry

    lax.fori_loop(0, 4, step_in, 0)
    send(at_send, a_own.at[h], S_SWAP_A, sibling)
    for k in range(2):
        swap_i(k).wait_recv()
    send(ibuf.at[0], ibuf.at[2], S_Y_I + 0, dev_y(1))
    send(ibuf.at[1], ibuf.at[3], S_Y_I + 1, dev_y(3))
    send(ibuf.at[1], ibuf.at[4], S_Y_I + 2, dev_y(1))
    send(ibuf.at[0], ibuf.at[5], S_Y_I + 3, dev_y(3))

    rows_of[2].wait()
    rows_of[3].wait()
    row = lax.broadcasted_iota(jnp.int32, (TOK, 256), 0)
    live = (row < lens[0]) | ((row >= RLEN) & (row < RLEN + lens[1]))
    live = live & ((row >= RLEN) | (row < lens[0]))

    def swap_g(k):
        part = gbuf.at[own_rows, pl.ds(pl.multiple_of(k * 256, 256), 256)]
        return copy(part, part, S_SWAP_G + k, sibling)

    def step_out(k, carry):
        load_out(k).wait()
        cols = pl.ds(pl.multiple_of(k * 256, 256), 256)
        r = dot(xout[...], bout[k], NN)
        gbuf[own_rows, cols] = jnp.where(live, r[:TOK], 0.0).astype(BF)
        swap_g(k).start()
        lb[h, v, u, :, cols] = r[TOK:].astype(BF)
        return carry

    lax.fori_loop(0, 4, step_out, 0)

    for d in range(1, 4):
        part = lb.at[h, v, u]
        send(part, part, S_L1 + d - 1, dev(d, 0))
    copy(at_send, a_own.at[1 - h], S_SWAP_A, sibling).wait_recv()
    others = [(du, dv) for du in range(4) for dv in range(4) if du or dv]
    for n, (du, dv) in enumerate(others):
        there = ((u + du) % 4) * 4 + (v + dv) % 4
        send(a_own.at[:, :, there], a_recv.at[me], S_A + n, dev(du, dv))
    a_recv[me] = a_own[:, :, me]

    def swap_g_wait(k, carry):
        swap_g(k).wait_recv()
        return carry

    lax.fori_loop(0, 4, swap_g_wait, 0)

    damp_1[0] = jnp.zeros((8, 128), F32)
    group = lax.broadcasted_iota(jnp.int32, (128, 128), 1) // RANK

    def place(i):
        first = (i < 2) * 1
        last = (i >= 6) * 1
        mid = 1 - first - last
        back = 1 - i % 2
        sigma = (y + last * 2 + mid * (back * 3 + (1 - back))) % 4
        k = (first + last) * (i % 2) + mid * ((i == 3) * 1 + (i == 4) * 1)
        return sigma * 2 + k

    def rows64(uu):
        return pl.ds(pl.multiple_of((uu % 4) * 64, 64), 64)

    def far_copies(i):
        over = (u + 2) % 4
        return (
            copy(snd.at[i, pl.ds(pl.multiple_of(over * 64, 64), 32)], far.at[i, 0], S_FAR + 2 * i, dev(1, 0)),
            copy(snd.at[i, pl.ds(pl.multiple_of(over * 64 + 32, 32), 32)], far.at[i, 1], S_FAR + 2 * i + 1, dev(3, 0)),
        )

    def near_copies(i):
        return (
            copy(snd.at[i, rows64(u + 1)], near.at[i, 0], S_NEAR + 2 * i, dev(1, 0)),
            copy(snd.at[i, rows64(u + 3)], near.at[i, 1], S_NEAR + 2 * i + 1, dev(3, 0)),
        )

    def far2_copies(i):
        over = (v + 2) % 4
        return (
            copy(snd2.at[i, over, :, pl.ds(0, 512)], far2.at[i, 0], S_FAR2 + 2 * i, dev(0, 1)),
            copy(snd2.at[i, over, :, pl.ds(512, 512)], far2.at[i, 1], S_FAR2 + 2 * i + 1, dev(0, 3)),
        )

    def near2_copies(i):
        return (
            copy(snd2.at[i, (v + 1) % 4], near2.at[i, 0], S_NEAR2 + 2 * i, dev(0, 1)),
            copy(snd2.at[i, (v + 3) % 4], near2.at[i, 1], S_NEAR2 + 2 * i + 1, dev(0, 3)),
        )

    def relay(i):
        return copy(ibuf.at[i], ibuf.at[i + 4], S_Y_I + i + 2, dev_y(1 + 2 * (i - 2)))

    def stage_squares(i):
        @pl.when(i >= 2)
        def _():
            copy(ibuf.at[i], ibuf.at[i], S_Y_I + i - 2, dev_y(1)).wait_recv()

        @pl.when((i == 2) | (i == 3))
        def _():
            relay(i).start()

        def tile(t, total):
            cols = pl.ds(pl.multiple_of(t * 256, 256), 256)
            value = None
            for n in range(4):
                r = dot(ibuf[i, n * RLEN : (n + 1) * RLEN], gbuf[n * RLEN : (n + 1) * RLEN, cols], TN)
                value = r * r if value is None else value + r * r
            acc[i, :, cols] = value
            return total + value.reshape(32, 8, 256).sum(axis=0)

        total = lax.fori_loop(0, 4, tile, jnp.zeros((8, 256), F32))
        damp_1[0] += total[:, :128] + total[:, 128:]
        over = rows64(u + 2)
        snd[i, over] = acc[i, over].astype(BF)
        for c in far_copies(i):
            c.start()

    def stage_near(i):
        for c in far_copies(i):
            c.wait_recv()
        a = pl.multiple_of(((u + 1) % 4) * 64, 64)
        snd[i, pl.ds(a, 32)] = (acc[i, pl.ds(a, 32)] + far[i, 0].astype(F32)).astype(BF)
        snd[i, pl.ds(a + 32, 32)] = acc[i, pl.ds(a + 32, 32)].astype(BF)
        b = pl.multiple_of(((u + 3) % 4) * 64, 64)
        snd[i, pl.ds(b, 32)] = acc[i, pl.ds(b, 32)].astype(BF)
        snd[i, pl.ds(b + 32, 32)] = (acc[i, pl.ds(b + 32, 32)] + far[i, 1].astype(F32)).astype(BF)
        for c in near_copies(i):
            c.start()

    def own16(vv):
        return pl.ds(pl.multiple_of(u * 64 + (vv % 4) * 16, 16), 16)

    def stage_far2(i):
        for c in near_copies(i):
            c.wait_recv()
        acc[i, rows64(u)] += near[i, 0].astype(F32) + near[i, 1].astype(F32)
        snd2[i, (v + 2) % 4] = acc[i, own16(v + 2)].astype(BF)
        for c in far2_copies(i):
            c.start()

    def stage_near2(i):
        for c in far2_copies(i):
            c.wait_recv()
        a, b = (v + 1) % 4, (v + 3) % 4
        snd2[i, a, :, :512] = (acc[i, own16(a), :512] + far2[i, 0].astype(F32)).astype(BF)
        snd2[i, a, :, 512:] = acc[i, own16(a), 512:].astype(BF)
        snd2[i, b, :, :512] = acc[i, own16(b), :512].astype(BF)
        snd2[i, b, :, 512:] = (acc[i, own16(b), 512:] + far2[i, 1].astype(F32)).astype(BF)
        for c in near2_copies(i):
            c.start()

    def stage_last(i):
        for c in near2_copies(i):
            c.wait_recv()
        corr[place(i)] = acc[i, own16(v)] + near2[i, 0].astype(F32) + near2[i, 1].astype(F32)

    def query_second():
        for d in range(1, 4):
            part = lb.at[h, v, u]
            copy(part, part, S_L1 + d - 1, dev(d, 0)).wait_recv()
        for d in range(1, 4):
            part = lb.at[h, v]
            copy(part, part, S_L2 + d - 1, dev(0, d)).start()

    def query_third():
        for d in range(1, 4):
            part = lb.at[h, v]
            copy(part, part, S_L2 + d - 1, dev(0, d)).wait_recv()
        copy(lb.at[h], lb.at[h], S_LS, sibling).start()
        for n, (du, dv) in enumerate(others):
            copy(a_own.at[:, :, me], a_recv.at[me], S_A + n, dev(du, dv)).wait_recv()
        for other in range(2):
            for vv in range(4):
                same = 1 - (other - h) * (other - h)
                total = jnp.zeros((32, 128), F32)
                for uu in range(4):
                    slot = same * (uu * 4 + vv) + (1 - same) * (vv * 4 + uu)
                    total = total + a_recv[slot, other].reshape(32, 128).astype(F32)
                a4[y, other * 4 + vv] = total.astype(BF)
        for d in range(1, 4):
            copy(a4.at[y], a4.at[y], S_AY + d - 1, dev_y(d)).start()

    def lgroup(g):
        return lb[g // 4, g % 4].reshape(128, WIDTH)

    def query_products():
        copy(lb.at[h], lb.at[1 - h], S_LS, sibling).wait_recv()

        def one(g, carry):
            rows = lgroup(g)
            full = dot(rows, rows, NT)
            packed = jnp.zeros((RANK, 128), F32)
            for q in range(4):
                packed = packed + jnp.where(lane // RANK == q, full[q * RANK : (q + 1) * RANK], 0.0)
            gram_s[g // 2, g % 2] = packed
            left_s[g // 2, :, pl.ds(pl.multiple_of((g % 2) * 128, 128), 128)] = dot(gbuf[own_rows], rows, NT)
            return carry

        lax.fori_loop(0, 8, one, 0)
        for d in (2, 1, 3):
            there = (y + d) % 4
            copy(gram_s.at[there], gram_r.at[d - 1], S_GRAM + d - 1, dev_y(d)).start()
        for d in (2, 1, 3):
            there = (y + d) % 4
            copy(left_s.at[there], left_r.at[d - 1], S_LEFT + d - 1, dev_y(d)).start()

    line = [(dy, dh) for dy in range(4) for dh in range(2) if dy or dh]

    def damping_first():
        for n, (dy, dh) in enumerate(line):
            copy(damp_1.at[0], damp_1.at[1 + n], S_D1 + n, dev_y(dy, dh)).start()

    def damping_second():
        for n, (dy, dh) in enumerate(line):
            copy(damp_1.at[0], damp_1.at[1 + n], S_D1 + n, dev_y(dy, dh)).wait_recv()
        damp_2[0] = damp_1[...].sum(axis=0)
        for n, (du, dv) in enumerate(others):
            copy(damp_2.at[0], damp_2.at[1 + n], S_D2 + n, dev(du, dv)).start()

    def gram_inverse():
        for d in range(1, 4):
            copy(gram_s.at[y], gram_r.at[d - 1], S_GRAM + d - 1, dev_y(d)).wait_recv()
        gram = gram_s[y] + gram_r[0] + gram_r[1] + gram_r[2]
        lane2 = lax.broadcasted_iota(jnp.int32, (128, 128), 1)
        sub2 = lax.broadcasted_iota(jnp.int32, (128, 128), 0)
        fold = ((sub2 % RANK == lane2) & (lane2 < RANK)).astype(F32)
        block = sub2 // RANK == lane2 // RANK
        wide = []
        for e in range(2):
            tall = jnp.concatenate([gram[e]] * 4, axis=0)
            wide.append(dot(jnp.where(block, tall, 0.0), fold, NN, HIGH).reshape(4, RANK, 128))
        w = jnp.concatenate(wide, axis=0)
        li = lax.broadcasted_iota(jnp.int32, (8, RANK, 128), 2)
        ri = lax.broadcasted_iota(jnp.int32, (8, RANK, 128), 1)
        w = w + jnp.where(li == ri, ridge_share * DIM, 0.0)

        def sweep(k, w):
            at_k = li == k
            col = jnp.where(at_k, w, 0.0).sum(axis=2, keepdims=True)
            rowk = jnp.where(ri == k, w, 0.0).sum(axis=1, keepdims=True)
            pivot = jnp.where(at_k[:, :1], rowk, 0.0).sum(axis=2, keepdims=True)
            rowk = jnp.where(at_k[:, :1], 1.0, rowk) / pivot
            return jnp.where(ri == k, rowk, jnp.where(at_k, 0.0, w) - col * rowk)

        w = lax.fori_loop(0, RANK, sweep, w)
        for e in range(2):
            flat = w[e * 4 : (e + 1) * 4].reshape(128, 128)
            inv_bd[e] = jnp.where(block, dot(flat, fold, NT, HIGH), 0.0)

    def left_sum():
        for d in range(1, 4):
            copy(left_s.at[y], left_r.at[d - 1], S_LEFT + d - 1, dev_y(d)).wait_recv()
        left_f[own_rows] = left_s[y] + left_r[0] + left_r[1] + left_r[2]
        copy(left_f.at[own_rows], left_f.at[own_rows], S_LEFTS, sibling).start()

    def step(i, carry):
        @pl.when(i < PARTS)
        def _():
            stage_squares(i)

        @pl.when((i >= 1) & (i < PARTS + 1))
        def _():
            stage_near(i - 1)

        @pl.when((i >= 2) & (i < PARTS + 2))
        def _():
            stage_far2(i - 2)

        @pl.when((i >= 3) & (i < PARTS + 3))
        def _():
            stage_near2(i - 3)

        @pl.when(i >= 4)
        def _():
            stage_last(i - 4)

        pl.when(i == 1)(query_second)
        pl.when(i == 3)(query_third)
        pl.when(i == 5)(query_products)
        pl.when(i == 7)(damping_first)

        @pl.when(i == 8)
        def _():
            gram_inverse()
            damping_second()

        pl.when(i == 9)(left_sum)
        return carry

    lax.fori_loop(0, PARTS + 4, step, 0)

    for n, (du, dv) in enumerate(others):
        copy(damp_2.at[0], damp_2.at[1 + n], S_D2 + n, dev(du, dv)).wait_recv()
    total = jnp.sum(damp_2[...])
    damping = damping_share * (total / 64.0 / (DIM * DIM)) + epsilon_add
    corr[...] = 1.0 / (corr[...] / 64.0 + damping)
    for d in range(1, 4):
        copy(a4.at[y], a4.at[y], S_AY + d - 1, dev_y(d)).wait_recv()

    def solve_group(g):
        a = a4[:, g].reshape(128, 128)
        a_all = jnp.concatenate([jnp.where(group == q, a, jnp.zeros_like(a)) for q in range(4)], axis=0)

        def tile(t, p):
            cols = pl.ds(pl.multiple_of(t * 256, 256), 256)
            rows = lb[g // 4, g % 4, :, :, cols].reshape(128, 256)
            rotated = dot(a_all, rows, NN)
            weight = corr[:, :, cols].reshape(1, 128, 256)
            scaled = (rotated.reshape(4, 128, 256) * weight).reshape(512, 256).astype(BF)
            return p + dot(scaled, rows, NT)

        p = lax.fori_loop(0, 4, tile, jnp.zeros((512, 128), F32))
        packed = jnp.zeros((128, 128), F32)
        for q in range(4):
            packed = packed + jnp.where(group == q, p[q * 128 : (q + 1) * 128], 0.0)
        proj_s[g // 2, g % 2] = packed

    def proj_copy(d):
        there = (y + d) % 4
        return copy(proj_s.at[there], proj_r.at[d - 1], S_PROJ + d - 1, dev_y(d))

    def solve_plane(n, carry):
        d = (n == 0) * 2 + (n == 1) * 1 + (n == 2) * 3
        there = (y + d) % 4
        solve_group(there * 2)
        solve_group(there * 2 + 1)

        @pl.when(n < 3)
        def _():
            proj_copy(d).start()

        return carry

    lax.fori_loop(0, 4, solve_plane, 0)
    for d in range(1, 4):
        proj_copy(d).wait_recv()
    mine = pl.ds(pl.multiple_of(me * 16, 16), 16)
    for e in range(2):
        whole = proj_s[y, e] + proj_r[0, e] + proj_r[1, e] + proj_r[2, e]
        solved = dot(whole, inv_bd[e], NN, HIGH).astype(BF)
        sb[:, mine, e * 128 : (e + 1) * 128] = solved.reshape(PARTS, 16, 128)

    def solved_first(d):
        return copy(sb.at[:, mine], sb.at[:, mine], S_S1 + d - 1, dev(0, d))

    def solved_second(d):
        part = sb.at[:, pl.ds(pl.multiple_of(u * 64, 64), 64)]
        return copy(part, part, S_S2 + d - 1, dev(d, 0))

    for d in range(1, 4):
        solved_first(d).start()
    for d in range(1, 4):
        solved_first(d).wait_recv()
    for d in range(1, 4):
        solved_second(d).start()
    copy(left_f.at[own_rows], left_f.at[own_rows], S_LEFTS, sibling).wait_recv()
    for d in range(1, 4):
        solved_second(d).wait_recv()

    def right_part(i, total):
        return total + dot(ibuf[i], sb[place(i)], NN)

    right = lax.fori_loop(0, PARTS, right_part, jnp.zeros((2 * TOK, 256), F32))
    joined = (left_f[...] * right).reshape(4, RLEN, 256).sum(axis=1)
    fin[y, h] = jnp.concatenate([joined, jnp.zeros((4, 256), F32)], axis=0)
    for n, (dy, dh) in enumerate(line):
        copy(fin.at[y, h], fin.at[y, h], S_FIN + n, dev_y(dy, dh)).start()
    p_of = lax.broadcasted_iota(jnp.int32, (256, 128), 0) // RANK
    q_of = lax.broadcasted_iota(jnp.int32, (256, 128), 1)
    for n, (dy, dh) in enumerate(line):
        copy(fin.at[y, h], fin.at[y, h], S_FIN + n, dev_y(dy, dh)).wait_recv()
    scores = jnp.zeros((8, 128), F32)
    for plane in range(4):
        p = p_of + plane * 8
        hh, first, second = p // 16, p % 4, (p // 4) % 4
        xx = first * (1 - hh) + second * hh
        zz = second * (1 - hh) + first * hh
        pick = (q_of == xx * 8 + zz * 2 + hh).astype(F32)
        scores = scores + dot(fin[plane, 0] + fin[plane, 1], pick, NN, HIGH)
    scores = scores / RLEN
    out[...] = jnp.where(h == 0, scores[0:2, :32], scores[2:4, :32])

    for c in pending:
        c.wait_send()

    def leave(k, carry):
        @pl.when(k < 2)
        def _():
            swap_i(k).wait_send()
            relay(k + 2).wait_send()

        @pl.when(k < 4)
        def _():
            swap_g(k).wait_send()

        for c in far_copies(k) + near_copies(k) + far2_copies(k) + near2_copies(k):
            c.wait_send()
        return carry

    lax.fori_loop(0, PARTS, leave, 0)
    for d in range(1, 4):
        copy(lb.at[h, v], lb.at[h, v], S_L2 + d - 1, dev(0, d)).wait_send()
        copy(a4.at[y], a4.at[y], S_AY + d - 1, dev_y(d)).wait_send()
        copy(gram_s.at[y], gram_r.at[d - 1], S_GRAM + d - 1, dev_y(d)).wait_send()
        copy(left_s.at[y], left_r.at[d - 1], S_LEFT + d - 1, dev_y(d)).wait_send()
        proj_copy(d).wait_send()
        solved_first(d).wait_send()
        solved_second(d).wait_send()
    copy(lb.at[h], lb.at[h], S_LS, sibling).wait_send()
    copy(left_f.at[own_rows], left_f.at[own_rows], S_LEFTS, sibling).wait_send()
    for n, (dy, dh) in enumerate(line):
        copy(damp_1.at[0], damp_1.at[1 + n], S_D1 + n, dev_y(dy, dh)).wait_send()
        copy(fin.at[y, h], fin.at[y, h], S_FIN + n, dev_y(dy, dh)).wait_send()
    for n, (du, dv) in enumerate(others):
        copy(damp_2.at[0], damp_2.at[1 + n], S_D2 + n, dev(du, dv)).wait_send()


def shards(act, grad, lengths, basis_in, basis_out, query_act, query_grad):
    vm = pltpu.VMEM
    anywhere = pl.BlockSpec(memory_space=pl.ANY)
    return pl.pallas_call(
        kernel,
        out_shape=jax.ShapeDtypeStruct((2, 32), F32),
        in_specs=[anywhere, anywhere, pl.BlockSpec(memory_space=pltpu.SMEM)] + [anywhere] * 4,
        out_specs=pl.BlockSpec(memory_space=pltpu.VMEM),
        scratch_shapes=[
            vm((TOK + RANK, DIM), BF),
            vm((TOK + RANK, DIM), BF),
            vm((4, DIM, 256), BF),
            vm((4, DIM, 256), BF),
            vm((2, TOK, 256), BF),
            vm((PARTS, 2 * TOK, 256), BF),
            vm((2 * TOK, WIDTH), BF),
            vm((2, 4, 4, RANK, WIDTH), BF),
            vm((2, 16, 16, 128), BF),
            vm((2, 2, 16, 16, 128), BF),
            vm((16, 2, 2, 16, 128), BF),
            vm((4, 8, 32, 128), BF),
            vm((PARTS, 256, WIDTH), F32),
            vm((PARTS, 256, WIDTH), BF),
            vm((PARTS, 2, 32, WIDTH), BF),
            vm((PARTS, 2, 64, WIDTH), BF),
            vm((PARTS, 4, 16, WIDTH), BF),
            vm((PARTS, 2, 16, 512), BF),
            vm((PARTS, 2, 16, WIDTH), BF),
            vm((PARTS, 16, WIDTH), F32),
            vm((4, 2, RANK, 128), F32),
            vm((3, 2, RANK, 128), F32),
            vm((4, TOK, 256), F32),
            vm((3, TOK, 256), F32),
            vm((2 * TOK, 256), F32),
            vm((8, 8, 128), F32),
            vm((16, 8, 128), F32),
            vm((2, 128, 128), F32),
            vm((4, 2, 128, 128), F32),
            vm((3, 2, 128, 128), F32),
            vm((PARTS, 256, 256), BF),
            vm((4, 2, 8, 256), F32),
            pltpu.SemaphoreType.DMA((12,)),
            pltpu.SemaphoreType.DMA((N_SEM,)),
            pltpu.SemaphoreType.DMA((N_SEM,)),
        ],
        compiler_params=pltpu.CompilerParams(
            collective_id=0, has_side_effects=True, vmem_limit_bytes=60 * 2**20
        ),
    )(act, grad, lengths, basis_in, basis_out, query_act, query_grad)


def solution(mesh):
    return jax.shard_map(
        shards,
        mesh=mesh,
        in_specs=(
            P("dp", None),
            P("dp", None),
            P("dp"),
            P(None, "col"),
            P(None, "col"),
            P("dp", None),
            P("dp", None),
        ),
        out_specs=P("dp", None),
        check_vma=False,
    )
```

time: 416 us -> 111 us (0.27)
  waiting for transfers between devices: 291 us -> 0 us
  Pallas kernels: 0 us -> 110 us
  matrix products: 59.2 us -> 0 us
  blocking collectives: 20.2 us -> 0 us
  other arithmetic: 19.1 us -> 0 us
  between operations: 13.9 us -> 0.01 us
  local copies, waits for them, and re-layouts: 11.1 us -> 1.24 us
    psum x1 -> x0, waiting for transfers between devices: 152 us -> none  [shards(): corr = lax.psum(partial_value, 'dp')]
    all_gather x4 -> x0, waiting for transfers between devices: 139 us -> none  [the longest x1 67.4 us: shards(): pieces = lax.all_gather(solved, ('dp', 'col'), axis=0, tiled=True)]
    pallas_call x0 -> x1, Pallas kernels: none -> 110 us  [shards(): pl.pallas_call(kernel, out_shape=jax.ShapeDtypeStruct((2, 32), F32), in_s...]
    dot_general x10 -> x0, matrix products: 57.9 us -> none  [the longest x2 10.8 us: shards(): lax.dot_general(grad_rows, act_rows, (((0,), (0,)), ((), ())), preferred_...]
    reduce_sum x3 -> x0, other arithmetic: 10.9 us -> none  [the longest x1 10.7 us: shards(): grand_sum = lax.psum(jnp.sum(corr), 'col')]
    all_gather x1 -> x0, blocking collectives: 10.7 us -> none  [shards(): lax.all_gather(query_part, 'col', axis=1, tiled=True)]
    psum x1 -> x0, blocking collectives: 9.47 us -> none  [shards(): grand_sum = lax.psum(jnp.sum(corr), 'col')]
    dot_general x1 -> x0, local copies, waits for them, and re-layouts: 8.46 us -> none  [shards(): jnp.einsum('tca,dcma->tdm', in_split, pieces, preferred_element_type=jnp....]
  transfers between devices with their start and end apart: 5 -> 0, of which waited for: 5 -> 0; matrix products, arithmetic and copies ran while one was open for 14% -> 0% of each run, Pallas kernels for 0% -> 0%
where the time goes in v1:
time: 111 us
  Pallas kernels  110 us (99%)
  local copies, waits for them, and re-layouts  1.24 us (1%)
    pallas_call x1, Pallas kernels, shards(): pl.pallas_call(kernel, out_shape=jax.ShapeDtypeStruct((2, 32), F32), in_s...  110 us

profile of v1, /device:TPU:1, one launch (start us, length us, event | category | flops | bytes accessed | tf_op | source)
XLA Modules:
  0.0 111.3 jit_solution(12644094383549826211)
XLA Ops:
  0.0 110.1 %shard_map.73 = f32[2,32]{1,0:T(2,128)} custom-call(bf16[256,4096]{1,0:T(8,128)(2,1)} %act.1, bf16[256,4096]{1,0:T(8,128)(2,1)} %grad.1, s32[2]{0:T(128)} %lens.1, bf16[4096,1024]{1,0:T(8,128)(2,1)} %b_in.1, bf16[4096,1024]{1,0:T(8,128)(2,1)} %b_out.1, bf16[32,4096]{1,0:T(8,128)(2,1)} %q_act.1, bf16[32,4096]{1,0:T(8,128)(2,1)} %q_grad.1), custom_call_target="tpu_custom_call" | custom-call | tf_op jit(solution)/shard_map/pallas_call | solution.py:589
  110.1 1.2 %copy.9 = f32[2,32]{1,0:T(2,128)} copy(f32[2,32]{1,0:T(2,128)} %shard_map.73) | data formatting | bytes 512

commit v2 on v1

v2 whole, which is shorter than its diff:
```python
import functools

import jax
import jax.numpy as jnp
from jax import lax
from jax.experimental import pallas as pl
from jax.experimental.pallas import tpu as pltpu
from jax.sharding import PartitionSpec as P


RLEN = 128
RANK = 32
DIM = 4096
WIDTH = 1024
TOK = 256
PARTS = 8
damping_share = 0.1
ridge_share = 0.05
epsilon_add = 1e-06
BF = jnp.bfloat16
F32 = jnp.float32
MESH = pl.DeviceIdType.MESH
HIGH = lax.Precision.HIGHEST


def dot(a, b, dims, precision=None):
    return lax.dot_general(a, b, (dims, ((), ())), preferred_element_type=F32, precision=precision)


NN = ((1,), (0,))
TN = ((0,), (0,))
NT = ((1,), (1,))


class Slots:
    def __init__(self):
        self.count = 0

    def take(self, n):
        first = self.count
        self.count += n
        return first


SL = Slots()
S_SWAP_I = SL.take(2)
S_SWAP_A = SL.take(1)
S_SWAP_G = SL.take(1)
S_Y_I = SL.take(6)
S_L1 = SL.take(3)
S_L2 = SL.take(3)
S_LS = SL.take(1)
S_A1 = SL.take(3)
S_A2 = SL.take(3)
S_AY = SL.take(3)
S_FAR = SL.take(2 * PARTS)
S_NEAR = SL.take(2 * PARTS)
S_OUT2 = SL.take(3 * PARTS)
S_GRAM = SL.take(3)
S_LEFT = SL.take(3)
S_LEFTS = SL.take(1)
S_D1 = SL.take(7)
S_D2 = SL.take(3)
S_D3 = SL.take(3)
S_PROJ = SL.take(6)
S_S1 = SL.take(6)
S_S2 = SL.take(6)
S_FIN = SL.take(7)
N_SEM = SL.count


def kernel(
    act, grad, lens, b_in, b_out, q_act, q_grad,
    out,
    xin, xout, bin_, bout, send_i, ibuf, gbuf, lb, at_send, a_own, a_mid, a_recv, a4,
    acc, snd, far, near, snd2, got2, corr,
    gram_s, gram_r, left_s, left_r, left_f, damp_1, damp_2, damp_3, inv_bd, proj_s, proj_r, sb, pick, fin,
    load_sem, ss, rs,
):
    dp = lax.axis_index("dp")
    y = lax.axis_index("col")
    x, z, h = dp // 8, (dp // 2) % 4, dp % 2
    u = x * (1 - h) + z * h
    v = z * (1 - h) + x * h
    me = u * 4 + v

    def dev_xz(xx, zz, hh, yy):
        return ((xx % 4) * 8 + (zz % 4) * 2 + hh, yy % 4)

    def dev(du, dv):
        uu, vv = u + du, v + dv
        return dev_xz(uu * (1 - h) + vv * h, vv * (1 - h) + uu * h, h, y)

    def dev_y(dy, dh=0):
        return dev_xz(x, z, (h + dh) % 2, y + dy)

    sibling = dev_y(0, 1)
    pending = []

    def copy(src, dst, idx, to):
        return pltpu.make_async_remote_copy(
            src_ref=src, dst_ref=dst, send_sem=ss.at[idx], recv_sem=rs.at[idx], device_id=to, device_id_type=MESH
        )

    def send(src, dst, idx, to):
        c = copy(src, dst, idx, to)
        c.start()
        pending.append(c)

    def tile_in(k):
        half = (1 - h) * (1 - k // 2) + h * (k // 2)
        return half * 2 + k % 2

    def load_in(k):
        cols = pl.ds(pl.multiple_of(tile_in(k) * 256, 256), 256)
        return pltpu.make_async_copy(b_in.at[:, cols], bin_.at[k], load_sem.at[4 + k])

    def load_out(k):
        cols = pl.ds(pl.multiple_of(k * 256, 256), 256)
        return pltpu.make_async_copy(b_out.at[:, cols], bout.at[k], load_sem.at[8 + k])

    rows_of = [
        pltpu.make_async_copy(act, xin.at[pl.ds(0, TOK)], load_sem.at[0]),
        pltpu.make_async_copy(q_act, xin.at[pl.ds(TOK, RANK)], load_sem.at[1]),
        pltpu.make_async_copy(grad, xout.at[pl.ds(0, TOK)], load_sem.at[2]),
        pltpu.make_async_copy(q_grad, xout.at[pl.ds(TOK, RANK)], load_sem.at[3]),
    ]
    rows_of[2].start()
    rows_of[3].start()
    for k in range(4):
        load_out(k).start()
    rows_of[0].start()
    rows_of[1].start()
    for k in range(4):
        load_in(k).start()

    line = [(dy, dh) for dy in range(4) for dh in range(2) if dy or dh]
    barrier = pltpu.get_barrier_semaphore()
    peers = [dev(d, 0) for d in range(1, 4)] + [dev(0, d) for d in range(1, 4)] + [dev_y(dy, dh) for dy, dh in line]
    for to in peers:
        pl.semaphore_signal(barrier, inc=1, device_id=to, device_id_type=MESH)

    lane = lax.broadcasted_iota(jnp.int32, (RANK, 128), 1)
    spread = (lane == lax.broadcasted_iota(jnp.int32, (RANK, 128), 0) + RANK * u).astype(BF)

    own_rows = pl.ds(pl.multiple_of(h * TOK, TOK), TOK)

    rows_of[2].wait()
    rows_of[3].wait()
    row = lax.broadcasted_iota(jnp.int32, (TOK, 256), 0)
    live = (row < lens[0]) | ((row >= RLEN) & (row < RLEN + lens[1]))

    def step_out(k, carry):
        load_out(k).wait()
        cols = pl.ds(pl.multiple_of(k * 256, 256), 256)
        r = dot(xout[...], bout[k], NN)
        gbuf[own_rows, cols] = jnp.where(live, r[:TOK], 0.0).astype(BF)
        lb[h, v, u, :, cols] = r[TOK:].astype(BF)
        return carry

    lax.fori_loop(0, 4, step_out, 0)

    rows_of[0].wait()
    rows_of[1].wait()

    def swap_i(k):
        return copy(send_i.at[k], ibuf.at[k, own_rows], S_SWAP_I + k, sibling)

    def step_in(k, carry):
        load_in(k).wait()
        r = dot(xin[...], bin_[k], NN).astype(BF)
        at = dot(r[TOK:], spread, TN).astype(BF).reshape(16, 16, 128)

        @pl.when(k < 2)
        def _():
            send_i[k] = r[:TOK]
            at_send[k] = at

        @pl.when(k >= 2)
        def _():
            ibuf[k - 2, own_rows] = r[:TOK]
            a_own[h, k - 2] = at

        return carry

    lax.fori_loop(0, 2, step_in, 0)
    pl.semaphore_wait(barrier, len(peers))
    for d in range(1, 4):
        part = lb.at[h, v, u]
        send(part, part, S_L1 + d - 1, dev(d, 0))
    for k in range(2):
        pending.append(swap_i(k))
        pending[-1].start()
    send(at_send, a_own.at[h], S_SWAP_A, sibling)
    send(gbuf.at[own_rows], gbuf.at[own_rows], S_SWAP_G, sibling)
    lax.fori_loop(2, 4, step_in, 0)
    for k in range(2):
        swap_i(k).wait_recv()
    send(ibuf.at[0], ibuf.at[2], S_Y_I + 0, dev_y(1))
    send(ibuf.at[1], ibuf.at[3], S_Y_I + 1, dev_y(3))
    send(ibuf.at[1], ibuf.at[4], S_Y_I + 2, dev_y(1))
    send(ibuf.at[0], ibuf.at[5], S_Y_I + 3, dev_y(3))

    copy(at_send, a_own.at[1 - h], S_SWAP_A, sibling).wait_recv()
    for d in range(1, 4):
        there = pl.ds(((u + d) % 4) * 4, 4)
        send(a_own.at[:, :, there], a_mid.at[u], S_A1 + d - 1, dev(d, 0))
    a_mid[u] = a_own[:, :, pl.ds(u * 4, 4)]
    for d in range(1, 4):
        part = lb.at[h, v, u]
        copy(part, part, S_L1 + d - 1, dev(d, 0)).wait_recv()
    for d in range(1, 4):
        send(lb.at[h, v], lb.at[h, v], S_L2 + d - 1, dev(0, d))
    copy(gbuf.at[own_rows], gbuf.at[own_rows], S_SWAP_G, sibling).wait_recv()

    damp_1[0] = jnp.zeros((8, 128), F32)
    group = lax.broadcasted_iota(jnp.int32, (128, 128), 1) // RANK

    def place(i):
        first = (i < 2) * 1
        last = (i >= 6) * 1
        mid = 1 - first - last
        back = 1 - i % 2
        sigma = (y + last * 2 + mid * (back * 3 + (1 - back))) % 4
        k = (first + last) * (i % 2) + mid * ((i == 3) * 1 + (i == 4) * 1)
        return sigma * 2 + k

    def rows64(uu):
        return pl.ds(pl.multiple_of((uu % 4) * 64, 64), 64)

    def far_copies(i):
        over = (u + 2) % 4
        return (
            copy(snd.at[i, pl.ds(pl.multiple_of(over * 64, 64), 32)], far.at[i, 0], S_FAR + 2 * i, dev(1, 0)),
            copy(snd.at[i, pl.ds(pl.multiple_of(over * 64 + 32, 32), 32)], far.at[i, 1], S_FAR + 2 * i + 1, dev(3, 0)),
        )

    def near_copies(i):
        return (
            copy(snd.at[i, rows64(u + 1)], near.at[i, 0], S_NEAR + 2 * i, dev(1, 0)),
            copy(snd.at[i, rows64(u + 3)], near.at[i, 1], S_NEAR + 2 * i + 1, dev(3, 0)),
        )

    def out2_copies(i):
        return [
            copy(snd2.at[i, (v + d) % 4], got2.at[i, d - 1], S_OUT2 + 3 * i + d - 1, dev(0, d)) for d in (2, 1, 3)
        ]

    def relay(i):
        return copy(ibuf.at[i], ibuf.at[i + 4], S_Y_I + i + 2, dev_y(1 + 2 * (i - 2)))

    def stage_squares(i):
        @pl.when(i >= 2)
        def _():
            copy(ibuf.at[i], ibuf.at[i], S_Y_I + i - 2, dev_y(1)).wait_recv()

        @pl.when((i == 2) | (i == 3))
        def _():
            relay(i).start()

        for n in range(4):
            r = dot(ibuf[i, n * RLEN : (n + 1) * RLEN], gbuf[n * RLEN : (n + 1) * RLEN], TN)
            if n == 0:
                acc[i] = r * r
            else:
                acc[i] += r * r
        total = acc[i].reshape(32, 8, WIDTH).sum(axis=0)
        for n in range(WIDTH // 128):
            damp_1[0] += total[:, n * 128 : (n + 1) * 128]
        over = rows64(u + 2)
        snd[i, over] = acc[i, over].astype(BF)
        for c in far_copies(i):
            c.start()

    def stage_near(i):
        for c in far_copies(i):
            c.wait_recv()
        a = pl.multiple_of(((u + 1) % 4) * 64, 64)
        snd[i, pl.ds(a, 32)] = (acc[i, pl.ds(a, 32)] + far[i, 0].astype(F32)).astype(BF)
        snd[i, pl.ds(a + 32, 32)] = acc[i, pl.ds(a + 32, 32)].astype(BF)
        b = pl.multiple_of(((u + 3) % 4) * 64, 64)
        snd[i, pl.ds(b, 32)] = acc[i, pl.ds(b, 32)].astype(BF)
        snd[i, pl.ds(b + 32, 32)] = (acc[i, pl.ds(b + 32, 32)] + far[i, 1].astype(F32)).astype(BF)
        for c in near_copies(i):
            c.start()

    def own16(vv):
        return pl.ds(pl.multiple_of(u * 64 + (vv % 4) * 16, 16), 16)

    def stage_out2(i):
        for c in near_copies(i):
            c.wait_recv()
        mine64 = rows64(u)
        total = acc[i, mine64] + near[i, 0].astype(F32) + near[i, 1].astype(F32)
        acc[i, mine64] = total
        snd2[i] = total.astype(BF).reshape(4, 16, WIDTH)
        for c in out2_copies(i):
            c.start()

    def stage_last(i, carry):
        for c in out2_copies(i):
            c.wait_recv()
        got = got2[i, 0].astype(F32) + got2[i, 1].astype(F32) + got2[i, 2].astype(F32)
        corr[place(i)] = 1.0 / ((acc[i, own16(v)] + got) / 64.0 + damping)
        return carry

    def query_second():
        for d in range(1, 4):
            copy(a_own.at[:, :, pl.ds(0, 4)], a_mid.at[u], S_A1 + d - 1, dev(d, 0)).wait_recv()
        for d in range(1, 4):
            copy(a_mid.at[:, :, :, (v + d) % 4], a_recv.at[v], S_A2 + d - 1, dev(0, d)).start()
        a_recv[v] = a_mid[:, :, :, v]

    def query_third():
        for d in range(1, 4):
            copy(lb.at[h, v], lb.at[h, v], S_L2 + d - 1, dev(0, d)).wait_recv()
        copy(lb.at[h], lb.at[h], S_LS, sibling).start()
        for d in range(1, 4):
            copy(a_mid.at[:, :, :, v], a_recv.at[v], S_A2 + d - 1, dev(0, d)).wait_recv()
        for other in range(2):
            for vv in range(4):
                same = 1 - (other - h) * (other - h)
                total = jnp.zeros((32, 128), F32)
                for uu in range(4):
                    first = same * vv + (1 - same) * uu
                    second = same * uu + (1 - same) * vv
                    total = total + a_recv[first, second, other].reshape(32, 128).astype(F32)
                a4[y, other * 4 + vv] = total.astype(BF)
        for d in range(1, 4):
            copy(a4.at[y], a4.at[y], S_AY + d - 1, dev_y(d)).start()

    def query_products():
        copy(lb.at[h], lb.at[1 - h], S_LS, sibling).wait_recv()

        def one(yy, carry):
            rows = lb[yy // 2, pl.ds((yy % 2) * 2, 2)].reshape(256, WIDTH)
            left_s[yy] = dot(gbuf[own_rows], rows, NT)
            full = dot(rows, rows, NT)
            for e in range(2):
                packed = jnp.zeros((RANK, 128), F32)
                for q in range(4):
                    at = e * 128 + q * RANK
                    packed = packed + jnp.where(lane // RANK == q, full[at : at + RANK, e * 128 : e * 128 + 128], 0.0)
                gram_s[yy, e] = packed
            return carry

        lax.fori_loop(0, 4, one, 0)
        for d in (2, 1, 3):
            there = (y + d) % 4
            copy(gram_s.at[there], gram_r.at[d - 1], S_GRAM + d - 1, dev_y(d)).start()
        for d in (2, 1, 3):
            there = (y + d) % 4
            copy(left_s.at[there], left_r.at[d - 1], S_LEFT + d - 1, dev_y(d)).start()

    def damping_first():
        for n, (dy, dh) in enumerate(line):
            copy(damp_1.at[0], damp_1.at[1 + n], S_D1 + n, dev_y(dy, dh)).start()

    def damping_second():
        for n, (dy, dh) in enumerate(line):
            copy(damp_1.at[0], damp_1.at[1 + n], S_D1 + n, dev_y(dy, dh)).wait_recv()
        damp_2[0] = damp_1[...].sum(axis=0)
        for d in range(1, 4):
            copy(damp_2.at[0], damp_2.at[d], S_D2 + d - 1, dev(d, 0)).start()

    def damping_third():
        for d in range(1, 4):
            copy(damp_2.at[0], damp_2.at[d], S_D2 + d - 1, dev(d, 0)).wait_recv()
        damp_3[0] = damp_2[...].sum(axis=0)
        for d in range(1, 4):
            copy(damp_3.at[0], damp_3.at[d], S_D3 + d - 1, dev(0, d)).start()

    def gram_inverse():
        for d in range(1, 4):
            copy(gram_s.at[y], gram_r.at[d - 1], S_GRAM + d - 1, dev_y(d)).wait_recv()
        gram = gram_s[y] + gram_r[0] + gram_r[1] + gram_r[2]
        lane2 = lax.broadcasted_iota(jnp.int32, (128, 128), 1)
        sub2 = lax.broadcasted_iota(jnp.int32, (128, 128), 0)
        fold = ((sub2 % RANK == lane2) & (lane2 < RANK)).astype(F32)
        block = sub2 // RANK == lane2 // RANK
        wide = []
        for e in range(2):
            tall = jnp.concatenate([gram[e]] * 4, axis=0)
            wide.append(dot(jnp.where(block, tall, 0.0), fold, NN, HIGH).reshape(4, RANK, 128))
        w = jnp.concatenate(wide, axis=0)
        li = lax.broadcasted_iota(jnp.int32, (8, RANK, 128), 2)
        ri = lax.broadcasted_iota(jnp.int32, (8, RANK, 128), 1)
        w = w + jnp.where(li == ri, ridge_share * DIM, 0.0)

        def sweep(k, w):
            at_k = li == k
            col = jnp.where(at_k, w, 0.0).sum(axis=2, keepdims=True)
            rowk = jnp.where(ri == k, w, 0.0).sum(axis=1, keepdims=True)
            pivot = jnp.where(at_k[:, :1], rowk, 0.0).sum(axis=2, keepdims=True)
            rowk = jnp.where(at_k[:, :1], 1.0, rowk) / pivot
            return jnp.where(ri == k, rowk, jnp.where(at_k, 0.0, w) - col * rowk)

        w = lax.fori_loop(0, RANK, sweep, w)
        for e in range(2):
            flat = w[e * 4 : (e + 1) * 4].reshape(128, 128)
            inv_bd[e] = jnp.where(block, dot(flat, fold, NT, HIGH), 0.0)

    def left_sum():
        for d in range(1, 4):
            copy(left_s.at[y], left_r.at[d - 1], S_LEFT + d - 1, dev_y(d)).wait_recv()
        left_f[own_rows] = left_s[y] + left_r[0] + left_r[1] + left_r[2]
        copy(left_f.at[own_rows], left_f.at[own_rows], S_LEFTS, sibling).start()

    def selection():
        p = lax.broadcasted_iota(jnp.int32, (256, 128), 0) // RANK + y * 8
        hh, first, second = p // 16, p % 4, (p // 4) % 4
        xx = first * (1 - hh) + second * hh
        zz = second * (1 - hh) + first * hh
        pick[...] = (lax.broadcasted_iota(jnp.int32, (256, 128), 1) == xx * 8 + zz * 2 + hh).astype(F32)

    def step(i, carry):
        @pl.when(i < PARTS)
        def _():
            stage_squares(i)

        @pl.when((i >= 2) & (i < PARTS + 2))
        def _():
            stage_near(i - 2)

        @pl.when(i >= 4)
        def _():
            stage_out2(i - 4)

        pl.when(i == 1)(query_second)
        pl.when(i == 3)(query_third)
        pl.when(i == 5)(query_products)
        pl.when(i == 7)(damping_first)
        pl.when(i == 8)(damping_second)

        @pl.when(i == 9)
        def _():
            damping_third()
            gram_inverse()

        @pl.when(i == 10)
        def _():
            left_sum()
            selection()

        return carry

    lax.fori_loop(0, PARTS + 4, step, 0)

    for d in range(1, 4):
        copy(damp_3.at[0], damp_3.at[d], S_D3 + d - 1, dev(0, d)).wait_recv()
    damping = damping_share * (jnp.sum(damp_3[...]) / 64.0 / (DIM * DIM)) + epsilon_add
    for d in range(1, 4):
        copy(a4.at[y], a4.at[y], S_AY + d - 1, dev_y(d)).wait_recv()
    lax.fori_loop(0, PARTS, stage_last, 0)

    def proj_copy(e, d):
        there = (y + d) % 4
        return copy(proj_s.at[there, e], proj_r.at[d - 1, e], S_PROJ + 3 * e + d - 1, dev_y(d))

    def solve_group(n, carry):
        e, m = n // 4, n % 4
        d = (m == 0) * 2 + (m == 1) * 1 + (m == 2) * 3
        there = (y + d) % 4
        g = there * 2 + e
        a = a4[:, g].reshape(128, 128)
        a_all = jnp.concatenate([jnp.where(group == q, a, jnp.zeros_like(a)) for q in range(4)], axis=0)
        rows = lb[g // 4, g % 4].reshape(128, WIDTH)
        rotated = dot(a_all, rows, NN)
        weight = corr[...].reshape(1, 128, WIDTH)
        scaled = (rotated.reshape(4, 128, WIDTH) * weight).reshape(512, WIDTH).astype(BF)
        p = dot(scaled, rows, NT)
        packed = jnp.zeros((128, 128), F32)
        for q in range(4):
            packed = packed + jnp.where(group == q, p[q * 128 : (q + 1) * 128], 0.0)
        proj_s[there, e] = packed

        @pl.when(m < 3)
        def _():
            proj_copy(e, d).start()

        return carry

    lax.fori_loop(0, 8, solve_group, 0)

    mine = pl.ds(pl.multiple_of(me * 16, 16), 16)

    def solved_first(e, d):
        return copy(sb.at[e, :, mine], sb.at[e, :, mine], S_S1 + 3 * e + d - 1, dev(0, d))

    def solved_second(e, d):
        part = sb.at[e, :, pl.ds(pl.multiple_of(u * 64, 64), 64)]
        return copy(part, part, S_S2 + 3 * e + d - 1, dev(d, 0))

    for e in range(2):
        for d in range(1, 4):
            proj_copy(e, d).wait_recv()
        whole = proj_s[y, e] + proj_r[0, e] + proj_r[1, e] + proj_r[2, e]
        solved = dot(whole, inv_bd[e], NN, HIGH).astype(BF)
        sb[e, :, mine] = solved.reshape(PARTS, 16, 128)
        for d in (2, 1, 3):
            solved_first(e, d).start()
    for e in range(2):
        for d in range(1, 4):
            solved_first(e, d).wait_recv()
        for d in (2, 1, 3):
            solved_second(e, d).start()
    copy(left_f.at[own_rows], left_f.at[own_rows], S_LEFTS, sibling).wait_recv()

    for c in pending:
        c.wait_send()

    def leave(k, carry):
        @pl.when(k < 2)
        def _():
            relay(k + 2).wait_send()

        for c in far_copies(k) + near_copies(k):
            c.wait_send()
        for c in out2_copies(k):
            c.wait_send()
        return carry

    lax.fori_loop(0, PARTS, leave, 0)
    for d in range(1, 4):
        copy(a_mid.at[:, :, :, (v + d) % 4], a_recv.at[v], S_A2 + d - 1, dev(0, d)).wait_send()
        copy(a4.at[y], a4.at[y], S_AY + d - 1, dev_y(d)).wait_send()
        copy(gram_s.at[y], gram_r.at[d - 1], S_GRAM + d - 1, dev_y(d)).wait_send()
        copy(left_s.at[y], left_r.at[d - 1], S_LEFT + d - 1, dev_y(d)).wait_send()
        copy(damp_2.at[0], damp_2.at[d], S_D2 + d - 1, dev(d, 0)).wait_send()
        copy(damp_3.at[0], damp_3.at[d], S_D3 + d - 1, dev(0, d)).wait_send()
        for e in range(2):
            proj_copy(e, d).wait_send()
            solved_first(e, d).wait_send()
    copy(lb.at[h], lb.at[h], S_LS, sibling).wait_send()
    copy(left_f.at[own_rows], left_f.at[own_rows], S_LEFTS, sibling).wait_send()
    for n, (dy, dh) in enumerate(line):
        copy(damp_1.at[0], damp_1.at[1 + n], S_D1 + n, dev_y(dy, dh)).wait_send()

    joined = []
    for e in range(2):
        for d in range(1, 4):
            solved_second(e, d).wait_recv()

        def right_part(i, total, e=e):
            return total + dot(ibuf[i], sb[e, place(i)], NN)

        right = lax.fori_loop(0, PARTS, right_part, jnp.zeros((2 * TOK, 128), F32))
        joined.append((left_f[:, e * 128 : (e + 1) * 128] * right).reshape(4, RLEN, 128).sum(axis=1))
    joined = jnp.concatenate([jnp.concatenate(joined, axis=1), jnp.zeros((4, 256), F32)], axis=0)
    fin[y, h] = dot(joined, pick[...], NN, HIGH)
    for n, (dy, dh) in enumerate(line):
        copy(fin.at[y, h], fin.at[y, h], S_FIN + n, dev_y(dy, dh)).start()
    for n, (dy, dh) in enumerate(line):
        copy(fin.at[y, h], fin.at[y, h], S_FIN + n, dev_y(dy, dh)).wait_recv()
    scores = fin[...].reshape(8, 8, 128).sum(axis=0) / RLEN
    out[...] = jnp.where(h == 0, scores[0:2, :32], scores[2:4, :32])
    for e in range(2):
        for d in range(1, 4):
            solved_second(e, d).wait_send()
    for n, (dy, dh) in enumerate(line):
        copy(fin.at[y, h], fin.at[y, h], S_FIN + n, dev_y(dy, dh)).wait_send()


def shards(act, grad, lengths, basis_in, basis_out, query_act, query_grad):
    vm = pltpu.VMEM
    anywhere = pl.BlockSpec(memory_space=pl.ANY)
    return pl.pallas_call(
        kernel,
        out_shape=jax.ShapeDtypeStruct((2, 32), F32),
        in_specs=[anywhere, anywhere, pl.BlockSpec(memory_space=pltpu.SMEM)] + [anywhere] * 4,
        out_specs=pl.BlockSpec(memory_space=pltpu.VMEM),
        scratch_shapes=[
            vm((TOK + RANK, DIM), BF),
            vm((TOK + RANK, DIM), BF),
            vm((4, DIM, 256), BF),
            vm((4, DIM, 256), BF),
            vm((2, TOK, 256), BF),
            vm((PARTS, 2 * TOK, 256), BF),
            vm((2 * TOK, WIDTH), BF),
            vm((2, 4, 4, RANK, WIDTH), BF),
            vm((2, 16, 16, 128), BF),
            vm((2, 2, 16, 16, 128), BF),
            vm((4, 2, 2, 4, 16, 128), BF),
            vm((4, 4, 2, 2, 16, 128), BF),
            vm((4, 8, 32, 128), BF),
            vm((PARTS, 256, WIDTH), F32),
            vm((PARTS, 256, WIDTH), BF),
            vm((PARTS, 2, 32, WIDTH), BF),
            vm((PARTS, 2, 64, WIDTH), BF),
            vm((PARTS, 4, 16, WIDTH), BF),
            vm((PARTS, 3, 16, WIDTH), BF),
            vm((PARTS, 16, WIDTH), F32),
            vm((4, 2, RANK, 128), F32),
            vm((3, 2, RANK, 128), F32),
            vm((4, TOK, 256), F32),
            vm((3, TOK, 256), F32),
            vm((2 * TOK, 256), F32),
            vm((8, 8, 128), F32),
            vm((4, 8, 128), F32),
            vm((4, 8, 128), F32),
            vm((2, 128, 128), F32),
            vm((4, 2, 128, 128), F32),
            vm((3, 2, 128, 128), F32),
            vm((2, PARTS, 256, 128), BF),
            vm((256, 128), F32),
            vm((4, 2, 8, 128), F32),
            pltpu.SemaphoreType.DMA((12,)),
            pltpu.SemaphoreType.DMA((N_SEM,)),
            pltpu.SemaphoreType.DMA((N_SEM,)),
        ],
        compiler_params=pltpu.CompilerParams(
            collective_id=0, has_side_effects=True, vmem_limit_bytes=60 * 2**20
        ),
    )(act, grad, lengths, basis_in, basis_out, query_act, query_grad)


def solution(mesh):
    return jax.shard_map(
        shards,
        mesh=mesh,
        in_specs=(
            P("dp", None),
            P("dp", None),
            P("dp"),
            P(None, "col"),
            P(None, "col"),
            P("dp", None),
            P("dp", None),
        ),
        out_specs=P("dp", None),
        check_vma=False,
    )
```

time: 111 us -> 93.6 us (0.84)
  Pallas kernels: 110 us -> 92.2 us
    pallas_call x1, Pallas kernels: 110 us -> 92.2 us  [shards(): pl.pallas_call(kernel, out_shape=jax.ShapeDtypeStruct((2, 32), F32), in_s...]
where the time goes in v2:
time: 93.6 us; the launch traced here: 93.5 us
  Pallas kernels  92.2 us (99%)
  local copies, waits for them, and re-layouts  1.24 us (1%)
    pallas_call x1, Pallas kernels, shards(): pl.pallas_call(kernel, out_shape=jax.ShapeDtypeStruct((2, 32), F32), in_s...  92.2 us

profile of v2, /device:TPU:1, one launch (start us, length us, event | category | flops | bytes accessed | tf_op | source)
XLA Modules:
  0.0 93.5 jit_solution(6463532782330826018)
XLA Ops:
  0.0 92.2 %shard_map.73 = f32[2,32]{1,0:T(2,128)} custom-call(bf16[256,4096]{1,0:T(8,128)(2,1)} %act.1, bf16[256,4096]{1,0:T(8,128)(2,1)} %grad.1, s32[2]{0:T(128)} %lens.1, bf16[4096,1024]{1,0:T(8,128)(2,1)} %b_in.1, bf16[4096,1024]{1,0:T(8,128)(2,1)} %b_out.1, bf16[32,4096]{1,0:T(8,128)(2,1)} %q_act.1, bf16[32,4096]{1,0:T(8,128)(2,1)} %q_grad.1), custom_call_target="tpu_custom_call" | custom-call | tf_op jit(solution)/shard_map/pallas_call | solution.py:567
  92.2 1.2 %copy.9 = f32[2,32]{1,0:T(2,128)} copy(f32[2,32]{1,0:T(2,128)} %shard_map.73) | data formatting | bytes 512

commit v3 on v2

--- a/solution.py
+++ b/solution.py
@@ -13,6 +13,7 @@
 DIM = 4096
 WIDTH = 1024
 TOK = 256
+RING = 5
 PARTS = 8
 damping_share = 0.1
 ridge_share = 0.05
@@ -72,9 +73,9 @@
 def kernel(
     act, grad, lens, b_in, b_out, q_act, q_grad,
     out,
-    xin, xout, bin_, bout, send_i, ibuf, gbuf, lb, at_send, a_own, a_mid, a_recv, a4,
+    xin, xout, basis, send_i, ibuf, gbuf, lb, at_send, a_own, a_mid, a_recv, a4,
     acc, snd, far, near, snd2, got2, corr,
-    gram_s, gram_r, left_s, left_r, left_f, damp_1, damp_2, damp_3, inv_bd, proj_s, proj_r, sb, pick, fin,
+    gram_s, gram_r, left_s, left_r, left_f, damp_1, damp_2, damp_3, inv_w, inv_bd, rotated, proj_s, proj_r, sb, pick, fin,
     load_sem, ss, rs,
 ):
     dp = lax.axis_index("dp")
@@ -113,11 +114,11 @@
 
     def load_in(k):
         cols = pl.ds(pl.multiple_of(tile_in(k) * 256, 256), 256)
-        return pltpu.make_async_copy(b_in.at[:, cols], bin_.at[k], load_sem.at[4 + k])
+        return pltpu.make_async_copy(b_in.at[:, cols], basis.at[k], load_sem.at[4 + k])
 
     def load_out(k):
         cols = pl.ds(pl.multiple_of(k * 256, 256), 256)
-        return pltpu.make_async_copy(b_out.at[:, cols], bout.at[k], load_sem.at[8 + k])
+        return pltpu.make_async_copy(b_out.at[:, cols], basis.at[k], load_sem.at[8 + k])
 
     rows_of = [
         pltpu.make_async_copy(act, xin.at[pl.ds(0, TOK)], load_sem.at[0]),
@@ -131,8 +132,6 @@
         load_out(k).start()
     rows_of[0].start()
     rows_of[1].start()
-    for k in range(4):
-        load_in(k).start()
 
     line = [(dy, dh) for dy in range(4) for dh in range(2) if dy or dh]
     barrier = pltpu.get_barrier_semaphore()
@@ -153,47 +152,53 @@
     def step_out(k, carry):
         load_out(k).wait()
         cols = pl.ds(pl.multiple_of(k * 256, 256), 256)
-        r = dot(xout[...], bout[k], NN)
+        r = dot(xout[...], basis[k], NN)
         gbuf[own_rows, cols] = jnp.where(live, r[:TOK], 0.0).astype(BF)
         lb[h, v, u, :, cols] = r[TOK:].astype(BF)
+        load_in(k).start()
         return carry
 
     lax.fori_loop(0, 4, step_out, 0)
-
-    rows_of[0].wait()
-    rows_of[1].wait()
-
-    def swap_i(k):
-        return copy(send_i.at[k], ibuf.at[k, own_rows], S_SWAP_I + k, sibling)
-
-    def step_in(k, carry):
-        load_in(k).wait()
-        r = dot(xin[...], bin_[k], NN).astype(BF)
-        at = dot(r[TOK:], spread, TN).astype(BF).reshape(16, 16, 128)
-
-        @pl.when(k < 2)
-        def _():
-            send_i[k] = r[:TOK]
-            at_send[k] = at
-
-        @pl.when(k >= 2)
-        def _():
-            ibuf[k - 2, own_rows] = r[:TOK]
-            a_own[h, k - 2] = at
-
-        return carry
-
-    lax.fori_loop(0, 2, step_in, 0)
     pl.semaphore_wait(barrier, len(peers))
     for d in range(1, 4):
         part = lb.at[h, v, u]
         send(part, part, S_L1 + d - 1, dev(d, 0))
+    send(gbuf.at[own_rows], gbuf.at[own_rows], S_SWAP_G, sibling)
+
+    rows_of[0].wait()
+    rows_of[1].wait()
+
+    def swap_i(k):
+        return copy(send_i.at[k], ibuf.at[k, own_rows], S_SWAP_I + k, sibling)
+
+    def step_in(k, carry):
+        load_in(k).wait()
+        r = dot(xin[...], basis[k], NN).astype(BF)
+        at = dot(r[TOK:], spread, TN).astype(BF).reshape(16, 16, 128)
+
+        @pl.when(k < 2)
+        def _():
+            send_i[k] = r[:TOK]
+            at_send[k] = at
+
+        @pl.when(k >= 2)
+        def _():
+            ibuf[k - 2, own_rows] = r[:TOK]
+            a_own[h, k - 2] = at
+
+        return carry
+
+    lax.fori_loop(0, 2, step_in, 0)
     for k in range(2):
         pending.append(swap_i(k))
         pending[-1].start()
     send(at_send, a_own.at[h], S_SWAP_A, sibling)
-    send(gbuf.at[own_rows], gbuf.at[own_rows], S_SWAP_G, sibling)
     lax.fori_loop(2, 4, step_in, 0)
+    for d in range(1, 4):
+        part = lb.at[h, v, u]
+        copy(part, part, S_L1 + d - 1, dev(d, 0)).wait_recv()
+    for d in range(1, 4):
+        send(lb.at[h, v], lb.at[h, v], S_L2 + d - 1, dev(0, d))
     for k in range(2):
         swap_i(k).wait_recv()
     send(ibuf.at[0], ibuf.at[2], S_Y_I + 0, dev_y(1))
@@ -206,11 +211,6 @@
         there = pl.ds(((u + d) % 4) * 4, 4)
         send(a_own.at[:, :, there], a_mid.at[u], S_A1 + d - 1, dev(d, 0))
     a_mid[u] = a_own[:, :, pl.ds(u * 4, 4)]
-    for d in range(1, 4):
-        part = lb.at[h, v, u]
-        copy(part, part, S_L1 + d - 1, dev(d, 0)).wait_recv()
-    for d in range(1, 4):
-        send(lb.at[h, v], lb.at[h, v], S_L2 + d - 1, dev(0, d))
     copy(gbuf.at[own_rows], gbuf.at[own_rows], S_SWAP_G, sibling).wait_recv()
 
     damp_1[0] = jnp.zeros((8, 128), F32)
@@ -261,14 +261,14 @@
         for n in range(4):
             r = dot(ibuf[i, n * RLEN : (n + 1) * RLEN], gbuf[n * RLEN : (n + 1) * RLEN], TN)
             if n == 0:
-                acc[i] = r * r
+                acc[i % RING] = r * r
             else:
-                acc[i] += r * r
-        total = acc[i].reshape(32, 8, WIDTH).sum(axis=0)
+                acc[i % RING] += r * r
+        total = acc[i % RING].reshape(32, 8, WIDTH).sum(axis=0)
         for n in range(WIDTH // 128):
             damp_1[0] += total[:, n * 128 : (n + 1) * 128]
         over = rows64(u + 2)
-        snd[i, over] = acc[i, over].astype(BF)
+        snd[i, over] = acc[i % RING, over].astype(BF)
         for c in far_copies(i):
             c.start()
 
@@ -276,11 +276,11 @@
         for c in far_copies(i):
             c.wait_recv()
         a = pl.multiple_of(((u + 1) % 4) * 64, 64)
-        snd[i, pl.ds(a, 32)] = (acc[i, pl.ds(a, 32)] + far[i, 0].astype(F32)).astype(BF)
-        snd[i, pl.ds(a + 32, 32)] = acc[i, pl.ds(a + 32, 32)].astype(BF)
+        snd[i, pl.ds(a, 32)] = (acc[i % RING, pl.ds(a, 32)] + far[i, 0].astype(F32)).astype(BF)
+        snd[i, pl.ds(a + 32, 32)] = acc[i % RING, pl.ds(a + 32, 32)].astype(BF)
         b = pl.multiple_of(((u + 3) % 4) * 64, 64)
-        snd[i, pl.ds(b, 32)] = acc[i, pl.ds(b, 32)].astype(BF)
-        snd[i, pl.ds(b + 32, 32)] = (acc[i, pl.ds(b + 32, 32)] + far[i, 1].astype(F32)).astype(BF)
+        snd[i, pl.ds(b, 32)] = acc[i % RING, pl.ds(b, 32)].astype(BF)
+        snd[i, pl.ds(b + 32, 32)] = (acc[i % RING, pl.ds(b + 32, 32)] + far[i, 1].astype(F32)).astype(BF)
         for c in near_copies(i):
             c.start()
 
@@ -291,8 +291,9 @@
         for c in near_copies(i):
             c.wait_recv()
         mine64 = rows64(u)
-        total = acc[i, mine64] + near[i, 0].astype(F32) + near[i, 1].astype(F32)
-        acc[i, mine64] = total
+        total = acc[i % RING, mine64] + near[i, 0].astype(F32) + near[i, 1].astype(F32)
+        acc[i % RING, mine64] = total
+        corr[place(i)] = acc[i % RING, own16(v)]
         snd2[i] = total.astype(BF).reshape(4, 16, WIDTH)
         for c in out2_copies(i):
             c.start()
@@ -301,7 +302,7 @@
         for c in out2_copies(i):
             c.wait_recv()
         got = got2[i, 0].astype(F32) + got2[i, 1].astype(F32) + got2[i, 2].astype(F32)
-        corr[place(i)] = 1.0 / ((acc[i, own16(v)] + got) / 64.0 + damping)
+        corr[place(i)] = 1.0 / ((corr[place(i)] + got) / 64.0 + damping)
         return carry
 
     def query_second():
@@ -329,12 +330,14 @@
         for d in range(1, 4):
             copy(a4.at[y], a4.at[y], S_AY + d - 1, dev_y(d)).start()
 
-    def query_products():
+    def plane_rows(yy):
+        return lb[yy // 2, pl.ds((yy % 2) * 2, 2)].reshape(256, WIDTH)
+
+    def gram_products():
         copy(lb.at[h], lb.at[1 - h], S_LS, sibling).wait_recv()
 
         def one(yy, carry):
-            rows = lb[yy // 2, pl.ds((yy % 2) * 2, 2)].reshape(256, WIDTH)
-            left_s[yy] = dot(gbuf[own_rows], rows, NT)
+            rows = plane_rows(yy)
             full = dot(rows, rows, NT)
             for e in range(2):
                 packed = jnp.zeros((RANK, 128), F32)
@@ -348,9 +351,21 @@
         for d in (2, 1, 3):
             there = (y + d) % 4
             copy(gram_s.at[there], gram_r.at[d - 1], S_GRAM + d - 1, dev_y(d)).start()
+
+    def left_products():
+        def one(yy, carry):
+            left_s[yy] = dot(gbuf[own_rows], plane_rows(yy), NT)
+            return carry
+
+        lax.fori_loop(0, 4, one, 0)
         for d in (2, 1, 3):
             there = (y + d) % 4
             copy(left_s.at[there], left_r.at[d - 1], S_LEFT + d - 1, dev_y(d)).start()
+
+    def rotate(g):
+        a = a4[:, g].reshape(128, 128)
+        a_all = jnp.concatenate([jnp.where(group == q, a, jnp.zeros_like(a)) for q in range(4)], axis=0)
+        rotated[g] = dot(a_all, lb[g // 4, g % 4].reshape(128, WIDTH), NN)
 
     def damping_first():
         for n, (dy, dh) in enumerate(line):
@@ -370,14 +385,18 @@
         for d in range(1, 4):
             copy(damp_3.at[0], damp_3.at[d], S_D3 + d - 1, dev(0, d)).start()
 
-    def gram_inverse():
+    lane2 = lax.broadcasted_iota(jnp.int32, (128, 128), 1)
+    sub2 = lax.broadcasted_iota(jnp.int32, (128, 128), 0)
+
+    def fold_block():
+        fold = ((sub2 % RANK == lane2) & (lane2 < RANK)).astype(F32)
+        return fold, sub2 // RANK == lane2 // RANK
+
+    def gram_begin():
         for d in range(1, 4):
             copy(gram_s.at[y], gram_r.at[d - 1], S_GRAM + d - 1, dev_y(d)).wait_recv()
         gram = gram_s[y] + gram_r[0] + gram_r[1] + gram_r[2]
-        lane2 = lax.broadcasted_iota(jnp.int32, (128, 128), 1)
-        sub2 = lax.broadcasted_iota(jnp.int32, (128, 128), 0)
-        fold = ((sub2 % RANK == lane2) & (lane2 < RANK)).astype(F32)
-        block = sub2 // RANK == lane2 // RANK
+        fold, block = fold_block()
         wide = []
         for e in range(2):
             tall = jnp.concatenate([gram[e]] * 4, axis=0)
@@ -385,7 +404,11 @@
         w = jnp.concatenate(wide, axis=0)
         li = lax.broadcasted_iota(jnp.int32, (8, RANK, 128), 2)
         ri = lax.broadcasted_iota(jnp.int32, (8, RANK, 128), 1)
-        w = w + jnp.where(li == ri, ridge_share * DIM, 0.0)
+        inv_w[...] = w + jnp.where(li == ri, ridge_share * DIM, 0.0)
+
+    def gram_sweep(first):
+        li = lax.broadcasted_iota(jnp.int32, (8, RANK, 128), 2)
+        ri = lax.broadcasted_iota(jnp.int32, (8, RANK, 128), 1)
 
         def sweep(k, w):
             at_k = li == k
@@ -395,9 +418,12 @@
             rowk = jnp.where(at_k[:, :1], 1.0, rowk) / pivot
             return jnp.where(ri == k, rowk, jnp.where(at_k, 0.0, w) - col * rowk)
 
-        w = lax.fori_loop(0, RANK, sweep, w)
+        inv_w[...] = lax.fori_loop(first, first + 8, sweep, inv_w[...])
+
+    def gram_end():
+        fold, block = fold_block()
         for e in range(2):
-            flat = w[e * 4 : (e + 1) * 4].reshape(128, 128)
+            flat = inv_w[e * 4 : (e + 1) * 4].reshape(128, 128)
             inv_bd[e] = jnp.where(block, dot(flat, fold, NT, HIGH), 0.0)
 
     def left_sum():
@@ -414,32 +440,45 @@
         pick[...] = (lax.broadcasted_iota(jnp.int32, (256, 128), 1) == xx * 8 + zz * 2 + hh).astype(F32)
 
     def step(i, carry):
+        @pl.when((i >= 2) & (i < PARTS + 2))
+        def _():
+            stage_near(i - 2)
+
+        @pl.when(i >= 4)
+        def _():
+            stage_out2(i - 4)
+
         @pl.when(i < PARTS)
         def _():
             stage_squares(i)
-
-        @pl.when((i >= 2) & (i < PARTS + 2))
-        def _():
-            stage_near(i - 2)
-
-        @pl.when(i >= 4)
-        def _():
-            stage_out2(i - 4)
 
         pl.when(i == 1)(query_second)
         pl.when(i == 3)(query_third)
-        pl.when(i == 5)(query_products)
+        pl.when(i == 5)(gram_products)
+        pl.when(i == 6)(left_products)
         pl.when(i == 7)(damping_first)
+        pl.when(i == 7)(gram_begin)
+
+        @pl.when((i >= 7) & (i < 11))
+        def _():
+            gram_sweep((i - 7) * 8)
+
         pl.when(i == 8)(damping_second)
-
-        @pl.when(i == 9)
-        def _():
-            damping_third()
-            gram_inverse()
-
-        @pl.when(i == 10)
-        def _():
-            left_sum()
+        pl.when(i == 9)(damping_third)
+
+        @pl.when(i == 7)
+        def _():
+            for d in range(1, 4):
+                copy(a4.at[y], a4.at[y], S_AY + d - 1, dev_y(d)).wait_recv()
+
+        @pl.when((i >= 7) & (i < 11))
+        def _():
+            rotate((i - 7) * 2)
+            rotate((i - 7) * 2 + 1)
+
+        @pl.when(i == 11)
+        def _():
+            gram_end()
             selection()
 
         return carry
@@ -449,8 +488,6 @@
     for d in range(1, 4):
         copy(damp_3.at[0], damp_3.at[d], S_D3 + d - 1, dev(0, d)).wait_recv()
     damping = damping_share * (jnp.sum(damp_3[...]) / 64.0 / (DIM * DIM)) + epsilon_add
-    for d in range(1, 4):
-        copy(a4.at[y], a4.at[y], S_AY + d - 1, dev_y(d)).wait_recv()
     lax.fori_loop(0, PARTS, stage_last, 0)
 
     def proj_copy(e, d):
@@ -462,12 +499,9 @@
         d = (m == 0) * 2 + (m == 1) * 1 + (m == 2) * 3
         there = (y + d) % 4
         g = there * 2 + e
-        a = a4[:, g].reshape(128, 128)
-        a_all = jnp.concatenate([jnp.where(group == q, a, jnp.zeros_like(a)) for q in range(4)], axis=0)
         rows = lb[g // 4, g % 4].reshape(128, WIDTH)
-        rotated = dot(a_all, rows, NN)
         weight = corr[...].reshape(1, 128, WIDTH)
-        scaled = (rotated.reshape(4, 128, WIDTH) * weight).reshape(512, WIDTH).astype(BF)
+        scaled = (rotated[g].reshape(4, 128, WIDTH) * weight).reshape(512, WIDTH).astype(BF)
         p = dot(scaled, rows, NT)
         packed = jnp.zeros((128, 128), F32)
         for q in range(4):
@@ -481,6 +515,7 @@
         return carry
 
     lax.fori_loop(0, 8, solve_group, 0)
+    left_sum()
 
     mine = pl.ds(pl.multiple_of(me * 16, 16), 16)
 
@@ -504,7 +539,6 @@
             solved_first(e, d).wait_recv()
         for d in (2, 1, 3):
             solved_second(e, d).start()
-    copy(left_f.at[own_rows], left_f.at[own_rows], S_LEFTS, sibling).wait_recv()
 
     for c in pending:
         c.wait_send()
@@ -536,15 +570,15 @@
     for n, (dy, dh) in enumerate(line):
         copy(damp_1.at[0], damp_1.at[1 + n], S_D1 + n, dev_y(dy, dh)).wait_send()
 
+    copy(left_f.at[own_rows], left_f.at[own_rows], S_LEFTS, sibling).wait_recv()
     joined = []
     for e in range(2):
         for d in range(1, 4):
             solved_second(e, d).wait_recv()
 
-        def right_part(i, total, e=e):
-            return total + dot(ibuf[i], sb[e, place(i)], NN)
-
-        right = lax.fori_loop(0, PARTS, right_part, jnp.zeros((2 * TOK, 128), F32))
+        right = jnp.zeros((2 * TOK, 128), F32)
+        for i in range(PARTS):
+            right = right + dot(ibuf[i], sb[e, place(i)], NN)
         joined.append((left_f[:, e * 128 : (e + 1) * 128] * right).reshape(4, RLEN, 128).sum(axis=1))
     joined = jnp.concatenate([jnp.concatenate(joined, axis=1), jnp.zeros((4, 256), F32)], axis=0)
     fin[y, h] = dot(joined, pick[...], NN, HIGH)
@@ -573,7 +607,6 @@
             vm((TOK + RANK, DIM), BF),
             vm((TOK + RANK, DIM), BF),
             vm((4, DIM, 256), BF),
-            vm((4, DIM, 256), BF),
             vm((2, TOK, 256), BF),
             vm((PARTS, 2 * TOK, 256), BF),
             vm((2 * TOK, WIDTH), BF),
@@ -583,7 +616,7 @@
             vm((4, 2, 2, 4, 16, 128), BF),
             vm((4, 4, 2, 2, 16, 128), BF),
             vm((4, 8, 32, 128), BF),
-            vm((PARTS, 256, WIDTH), F32),
+            vm((RING, 256, WIDTH), F32),
             vm((PARTS, 256, WIDTH), BF),
             vm((PARTS, 2, 32, WIDTH), BF),
             vm((PARTS, 2, 64, WIDTH), BF),
@@ -598,7 +631,9 @@
             vm((8, 8, 128), F32),
             vm((4, 8, 128), F32),
             vm((4, 8, 128), F32),
+            vm((8, RANK, 128), F32),
             vm((2, 128, 128), F32),
+            vm((8, 512, WIDTH), F32),
             vm((4, 2, 128, 128), F32),
             vm((3, 2, 128, 128), F32),
             vm((2, PARTS, 256, 128), BF),

time: 93.6 us -> 92.7 us (level)
  no operation moved by 1% of the time
where the time goes in v3:
time: 92.7 us; the launch traced here: 92.6 us
  Pallas kernels  91.3 us (98%)
  local copies, waits for them, and re-layouts  1.24 us (1%)
    pallas_call x1, Pallas kernels, shards(): pl.pallas_call(kernel, out_shape=jax.ShapeDtypeStruct((2, 32), F32), in_s...  91.3 us

profile of v3, /device:TPU:1, one launch (start us, length us, event | category | flops | bytes accessed | tf_op | source)
XLA Modules:
  0.0 92.6 jit_solution(5867753803846583669)
XLA Ops:
  0.0 91.3 %shard_map.73 = f32[2,32]{1,0:T(2,128)} custom-call(bf16[256,4096]{1,0:T(8,128)(2,1)} %act.1, bf16[256,4096]{1,0:T(8,128)(2,1)} %grad.1, s32[2]{0:T(128)} %lens.1, bf16[4096,1024]{1,0:T(8,128)(2,1)} %b_in.1, bf16[4096,1024]{1,0:T(8,128)(2,1)} %b_out.1, bf16[32,4096]{1,0:T(8,128)(2,1)} %q_act.1, bf16[32,4096]{1,0:T(8,128)(2,1)} %q_grad.1), custom_call_target="tpu_custom_call" | custom-call | tf_op jit(solution)/shard_map/pallas_call | solution.py:601
  91.4 1.2 %copy.9 = f32[2,32]{1,0:T(2,128)} copy(f32[2,32]{1,0:T(2,128)} %shard_map.73) | data formatting | bytes 512

commit v4 on v3

--- a/solution.py
+++ b/solution.py
@@ -439,8 +439,12 @@
         zz = second * (1 - hh) + first * hh
         pick[...] = (lax.broadcasted_iota(jnp.int32, (256, 128), 1) == xx * 8 + zz * 2 + hh).astype(F32)
 
+    def rotate_ready():
+        for d in range(1, 4):
+            copy(a4.at[y], a4.at[y], S_AY + d - 1, dev_y(d)).wait_recv()
+
     def step(i, carry):
-        @pl.when((i >= 2) & (i < PARTS + 2))
+        @pl.when(i >= 2)
         def _():
             stage_near(i - 2)
 
@@ -448,42 +452,47 @@
         def _():
             stage_out2(i - 4)
 
-        @pl.when(i < PARTS)
-        def _():
-            stage_squares(i)
-
+        stage_squares(i)
         pl.when(i == 1)(query_second)
         pl.when(i == 3)(query_third)
-        pl.when(i == 5)(gram_products)
-        pl.when(i == 6)(left_products)
+        pl.when(i == 4)(gram_products)
+
+        @pl.when(i == 5)
+        def _():
+            left_products()
+            rotate_ready()
+
+        pl.when(i == 6)(gram_begin)
         pl.when(i == 7)(damping_first)
-        pl.when(i == 7)(gram_begin)
-
-        @pl.when((i >= 7) & (i < 11))
-        def _():
-            gram_sweep((i - 7) * 8)
-
-        pl.when(i == 8)(damping_second)
-        pl.when(i == 9)(damping_third)
-
-        @pl.when(i == 7)
-        def _():
-            for d in range(1, 4):
-                copy(a4.at[y], a4.at[y], S_AY + d - 1, dev_y(d)).wait_recv()
-
-        @pl.when((i >= 7) & (i < 11))
-        def _():
-            rotate((i - 7) * 2)
-            rotate((i - 7) * 2 + 1)
-
-        @pl.when(i == 11)
-        def _():
-            gram_end()
-            selection()
+
+        @pl.when(i >= 6)
+        def _():
+            gram_sweep((i - 6) * 8)
+            rotate((i - 6) * 2)
+            rotate((i - 6) * 2 + 1)
 
         return carry
 
-    lax.fori_loop(0, PARTS + 4, step, 0)
+    lax.fori_loop(0, PARTS, step, 0)
+    stage_near(PARTS - 2)
+    stage_out2(PARTS - 4)
+    gram_sweep(16)
+    stage_near(PARTS - 1)
+    stage_out2(PARTS - 3)
+    damping_second()
+    gram_sweep(24)
+    stage_out2(PARTS - 2)
+    damping_third()
+
+    def rotate_rest(g, carry):
+        rotate(g)
+        return carry
+
+    lax.fori_loop(4, 6, rotate_rest, 0)
+    stage_out2(PARTS - 1)
+    lax.fori_loop(6, 8, rotate_rest, 0)
+    gram_end()
+    selection()
 
     for d in range(1, 4):
         copy(damp_3.at[0], damp_3.at[d], S_D3 + d - 1, dev(0, d)).wait_recv()

time: 92.7 us -> 90.7 us (0.978)
  Pallas kernels: 91.3 us -> 89.4 us
    pallas_call x1, Pallas kernels: 91.3 us -> 89.4 us  [shards(): pl.pallas_call(kernel, out_shape=jax.ShapeDtypeStruct((2, 32), F32), in_s...]
where the time goes in v4:
time: 90.7 us; the launch traced here: 90.6 us
  Pallas kernels  89.4 us (99%)
  local copies, waits for them, and re-layouts  1.24 us (1%)
    pallas_call x1, Pallas kernels, shards(): pl.pallas_call(kernel, out_shape=jax.ShapeDtypeStruct((2, 32), F32), in_s...  89.4 us

profile of v4, /device:TPU:1, one launch (start us, length us, event | category | flops | bytes accessed | tf_op | source)
XLA Modules:
  0.0 90.6 jit_solution(12023603317758768062)
XLA Ops:
  0.0 89.4 %shard_map.73 = f32[2,32]{1,0:T(2,128)} custom-call(bf16[256,4096]{1,0:T(8,128)(2,1)} %act.1, bf16[256,4096]{1,0:T(8,128)(2,1)} %grad.1, s32[2]{0:T(128)} %lens.1, bf16[4096,1024]{1,0:T(8,128)(2,1)} %b_in.1, bf16[4096,1024]{1,0:T(8,128)(2,1)} %b_out.1, bf16[32,4096]{1,0:T(8,128)(2,1)} %q_act.1, bf16[32,4096]{1,0:T(8,128)(2,1)} %q_grad.1), custom_call_target="tpu_custom_call" | custom-call | tf_op jit(solution)/shard_map/pallas_call | solution.py:610
  89.4 1.2 %copy.9 = f32[2,32]{1,0:T(2,128)} copy(f32[2,32]{1,0:T(2,128)} %shard_map.73) | data formatting | bytes 512

commit v5 on v4

--- a/solution.py
+++ b/solution.py
@@ -406,7 +406,7 @@
         ri = lax.broadcasted_iota(jnp.int32, (8, RANK, 128), 1)
         inv_w[...] = w + jnp.where(li == ri, ridge_share * DIM, 0.0)
 
-    def gram_sweep(first):
+    def gram_sweep(first, last):
         li = lax.broadcasted_iota(jnp.int32, (8, RANK, 128), 2)
         ri = lax.broadcasted_iota(jnp.int32, (8, RANK, 128), 1)
 
@@ -418,7 +418,7 @@
             rowk = jnp.where(at_k[:, :1], 1.0, rowk) / pivot
             return jnp.where(ri == k, rowk, jnp.where(at_k, 0.0, w) - col * rowk)
 
-        inv_w[...] = lax.fori_loop(first, first + 8, sweep, inv_w[...])
+        inv_w[...] = lax.fori_loop(first, last, sweep, inv_w[...])
 
     def gram_end():
         fold, block = fold_block()
@@ -455,42 +455,30 @@
         stage_squares(i)
         pl.when(i == 1)(query_second)
         pl.when(i == 3)(query_third)
-        pl.when(i == 4)(gram_products)
-
-        @pl.when(i == 5)
-        def _():
-            left_products()
-            rotate_ready()
-
-        pl.when(i == 6)(gram_begin)
+        pl.when(i == 5)(gram_products)
         pl.when(i == 7)(damping_first)
-
-        @pl.when(i >= 6)
-        def _():
-            gram_sweep((i - 6) * 8)
-            rotate((i - 6) * 2)
-            rotate((i - 6) * 2 + 1)
-
+        return carry
+
+    def rotate_some(g, carry):
+        rotate(g)
         return carry
 
     lax.fori_loop(0, PARTS, step, 0)
     stage_near(PARTS - 2)
     stage_out2(PARTS - 4)
-    gram_sweep(16)
+    left_products()
     stage_near(PARTS - 1)
     stage_out2(PARTS - 3)
     damping_second()
-    gram_sweep(24)
+    gram_begin()
+    gram_sweep(0, 12)
     stage_out2(PARTS - 2)
     damping_third()
-
-    def rotate_rest(g, carry):
-        rotate(g)
-        return carry
-
-    lax.fori_loop(4, 6, rotate_rest, 0)
+    rotate_ready()
+    lax.fori_loop(0, 3, rotate_some, 0)
     stage_out2(PARTS - 1)
-    lax.fori_loop(6, 8, rotate_rest, 0)
+    lax.fori_loop(3, 8, rotate_some, 0)
+    gram_sweep(12, 32)
     gram_end()
     selection()
 

time: 90.7 us -> 87.7 us (0.967)
  Pallas kernels: 89.4 us -> 86.3 us
    pallas_call x1, Pallas kernels: 89.4 us -> 86.3 us  [shards(): pl.pallas_call(kernel, out_shape=jax.ShapeDtypeStruct((2, 32), F32), in_s...]
where the time goes in v5:
time: 87.7 us; the launch traced here: 87.5 us
  Pallas kernels  86.3 us (98%)
  local copies, waits for them, and re-layouts  1.24 us (1%)
    pallas_call x1, Pallas kernels, shards(): pl.pallas_call(kernel, out_shape=jax.ShapeDtypeStruct((2, 32), F32), in_s...  86.3 us

profile of v5, /device:TPU:1, one launch (start us, length us, event | category | flops | bytes accessed | tf_op | source)
XLA Modules:
  0.0 87.5 jit_solution(890007320076978365)
XLA Ops:
  0.0 86.3 %shard_map.73 = f32[2,32]{1,0:T(2,128)} custom-call(bf16[256,4096]{1,0:T(8,128)(2,1)} %act.1, bf16[256,4096]{1,0:T(8,128)(2,1)} %grad.1, s32[2]{0:T(128)} %lens.1, bf16[4096,1024]{1,0:T(8,128)(2,1)} %b_in.1, bf16[4096,1024]{1,0:T(8,128)(2,1)} %b_out.1, bf16[32,4096]{1,0:T(8,128)(2,1)} %q_act.1, bf16[32,4096]{1,0:T(8,128)(2,1)} %q_grad.1), custom_call_target="tpu_custom_call" | custom-call | tf_op jit(solution)/shard_map/pallas_call | solution.py:598
  86.3 1.2 %copy.9 = f32[2,32]{1,0:T(2,128)} copy(f32[2,32]{1,0:T(2,128)} %shard_map.73) | data formatting | bytes 512

commit v6 on v5

--- a/solution.py
+++ b/solution.py
@@ -443,42 +443,43 @@
         for d in range(1, 4):
             copy(a4.at[y], a4.at[y], S_AY + d - 1, dev_y(d)).wait_recv()
 
-    def step(i, carry):
-        @pl.when(i >= 2)
-        def _():
-            stage_near(i - 2)
-
-        @pl.when(i >= 4)
-        def _():
-            stage_out2(i - 4)
-
-        stage_squares(i)
-        pl.when(i == 1)(query_second)
-        pl.when(i == 3)(query_third)
-        pl.when(i == 5)(gram_products)
-        pl.when(i == 7)(damping_first)
-        return carry
-
     def rotate_some(g, carry):
         rotate(g)
         return carry
 
-    lax.fori_loop(0, PARTS, step, 0)
-    stage_near(PARTS - 2)
-    stage_out2(PARTS - 4)
-    left_products()
-    stage_near(PARTS - 1)
-    stage_out2(PARTS - 3)
+    def step(p, carry):
+        stage_squares(2 * p)
+        stage_squares(2 * p + 1)
+
+        @pl.when(p >= 1)
+        def _():
+            stage_out2(2 * p - 2)
+            stage_out2(2 * p - 1)
+
+        pl.when(p == 0)(query_second)
+        pl.when(p == 1)(query_third)
+        pl.when(p == 2)(gram_products)
+
+        @pl.when(p == 3)
+        def _():
+            damping_first()
+            left_products()
+            rotate_ready()
+            lax.fori_loop(0, 4, rotate_some, 0)
+
+        stage_near(2 * p)
+        stage_near(2 * p + 1)
+        return carry
+
+    lax.fori_loop(0, PARTS // 2, step, 0)
     damping_second()
     gram_begin()
-    gram_sweep(0, 12)
+    gram_sweep(0, 16)
     stage_out2(PARTS - 2)
+    stage_out2(PARTS - 1)
     damping_third()
-    rotate_ready()
-    lax.fori_loop(0, 3, rotate_some, 0)
-    stage_out2(PARTS - 1)
-    lax.fori_loop(3, 8, rotate_some, 0)
-    gram_sweep(12, 32)
+    lax.fori_loop(4, 8, rotate_some, 0)
+    gram_sweep(16, 32)
     gram_end()
     selection()
 

time: 87.7 us -> 92.2 us (1.051)
  Pallas kernels: 86.3 us -> 90.9 us
    pallas_call x1, Pallas kernels: 86.3 us -> 90.9 us  [shards(): pl.pallas_call(kernel, out_shape=jax.ShapeDtypeStruct((2, 32), F32), in_s...]
where the time goes in v6:
time: 92.2 us; the launch traced here: 92.1 us
  Pallas kernels  90.9 us (99%)
  local copies, waits for them, and re-layouts  1.24 us (1%)
    pallas_call x1, Pallas kernels, shards(): pl.pallas_call(kernel, out_shape=jax.ShapeDtypeStruct((2, 32), F32), in_s...  90.9 us

profile of v6, /device:TPU:1, one launch (start us, length us, event | category | flops | bytes accessed | tf_op | source)
XLA Modules:
  0.0 92.1 jit_solution(11095231460839614877)
XLA Ops:
  0.0 90.9 %shard_map.73 = f32[2,32]{1,0:T(2,128)} custom-call(bf16[256,4096]{1,0:T(8,128)(2,1)} %act.1, bf16[256,4096]{1,0:T(8,128)(2,1)} %grad.1, s32[2]{0:T(128)} %lens.1, bf16[4096,1024]{1,0:T(8,128)(2,1)} %b_in.1, bf16[4096,1024]{1,0:T(8,128)(2,1)} %b_out.1, bf16[32,4096]{1,0:T(8,128)(2,1)} %q_act.1, bf16[32,4096]{1,0:T(8,128)(2,1)} %q_grad.1), custom_call_target="tpu_custom_call" | custom-call | tf_op jit(solution)/shard_map/pallas_call | solution.py:599
  90.9 1.2 %copy.9 = f32[2,32]{1,0:T(2,128)} copy(f32[2,32]{1,0:T(2,128)} %shard_map.73) | data formatting | bytes 512

commit v7 on v5

--- a/solution.py
+++ b/solution.py
@@ -444,15 +444,16 @@
             copy(a4.at[y], a4.at[y], S_AY + d - 1, dev_y(d)).wait_recv()
 
     def step(i, carry):
-        @pl.when(i >= 2)
-        def _():
-            stage_near(i - 2)
-
-        @pl.when(i >= 4)
-        def _():
-            stage_out2(i - 4)
+        @pl.when(i >= 3)
+        def _():
+            stage_near(i - 3)
+
+        @pl.when(i >= 5)
+        def _():
+            stage_out2(i - 5)
 
         stage_squares(i)
+
         pl.when(i == 1)(query_second)
         pl.when(i == 3)(query_third)
         pl.when(i == 5)(gram_products)
@@ -464,7 +465,9 @@
         return carry
 
     lax.fori_loop(0, PARTS, step, 0)
+    stage_near(PARTS - 3)
     stage_near(PARTS - 2)
+    stage_out2(PARTS - 5)
     stage_out2(PARTS - 4)
     left_products()
     stage_near(PARTS - 1)

time: 87.7 us -> 86 us (0.981)
  Pallas kernels: 86.3 us -> 84.7 us
    pallas_call x1, Pallas kernels: 86.3 us -> 84.7 us  [shards(): pl.pallas_call(kernel, out_shape=jax.ShapeDtypeStruct((2, 32), F32), in_s...]
where the time goes in v7:
time: 86 us; the launch traced here: 85.9 us
  Pallas kernels  84.7 us (98%)
  local copies, waits for them, and re-layouts  1.24 us (1%)
    pallas_call x1, Pallas kernels, shards(): pl.pallas_call(kernel, out_shape=jax.ShapeDtypeStruct((2, 32), F32), in_s...  84.7 us

profile of v7, /device:TPU:1, one launch (start us, length us, event | category | flops | bytes accessed | tf_op | source)
XLA Modules:
  0.0 85.9 jit_solution(13306357347124066122)
XLA Ops:
  0.0 84.7 %shard_map.73 = f32[2,32]{1,0:T(2,128)} custom-call(bf16[256,4096]{1,0:T(8,128)(2,1)} %act.1, bf16[256,4096]{1,0:T(8,128)(2,1)} %grad.1, s32[2]{0:T(128)} %lens.1, bf16[4096,1024]{1,0:T(8,128)(2,1)} %b_in.1, bf16[4096,1024]{1,0:T(8,128)(2,1)} %b_out.1, bf16[32,4096]{1,0:T(8,128)(2,1)} %q_act.1, bf16[32,4096]{1,0:T(8,128)(2,1)} %q_grad.1), custom_call_target="tpu_custom_call" | custom-call | tf_op jit(solution)/shard_map/pallas_call | solution.py:601
  84.7 1.2 %copy.9 = f32[2,32]{1,0:T(2,128)} copy(f32[2,32]{1,0:T(2,128)} %shard_map.73) | data formatting | bytes 512

commit v8 on v7

--- a/solution.py
+++ b/solution.py
@@ -469,10 +469,10 @@
     stage_near(PARTS - 2)
     stage_out2(PARTS - 5)
     stage_out2(PARTS - 4)
-    left_products()
     stage_near(PARTS - 1)
     stage_out2(PARTS - 3)
     damping_second()
+    left_products()
     gram_begin()
     gram_sweep(0, 12)
     stage_out2(PARTS - 2)

time: 86 us -> 86 us (level)
  no operation moved by 1% of the time
where the time goes in v8:
time: 86 us; the launch traced here: 85.9 us
  Pallas kernels  84.7 us (98%)
  local copies, waits for them, and re-layouts  1.24 us (1%)
    pallas_call x1, Pallas kernels, shards(): pl.pallas_call(kernel, out_shape=jax.ShapeDtypeStruct((2, 32), F32), in_s...  84.7 us

profile of v8, /device:TPU:1, one launch (start us, length us, event | category | flops | bytes accessed | tf_op | source)
XLA Modules:
  0.0 85.9 jit_solution(10436419262201859215)
XLA Ops:
  0.0 84.7 %shard_map.73 = f32[2,32]{1,0:T(2,128)} custom-call(bf16[256,4096]{1,0:T(8,128)(2,1)} %act.1, bf16[256,4096]{1,0:T(8,128)(2,1)} %grad.1, s32[2]{0:T(128)} %lens.1, bf16[4096,1024]{1,0:T(8,128)(2,1)} %b_in.1, bf16[4096,1024]{1,0:T(8,128)(2,1)} %b_out.1, bf16[32,4096]{1,0:T(8,128)(2,1)} %q_act.1, bf16[32,4096]{1,0:T(8,128)(2,1)} %q_grad.1), custom_call_target="tpu_custom_call" | custom-call | tf_op jit(solution)/shard_map/pallas_call | solution.py:601
  84.7 1.2 %copy.9 = f32[2,32]{1,0:T(2,128)} copy(f32[2,32]{1,0:T(2,128)} %shard_map.73) | data formatting | bytes 512
